TPU v7x, 32 devices: a whole 2x2x4 slice. The times are simulated.
32 devices in a mesh: expert: 8 (over z, core), dp: 4 (over y, x).
Axes of the slice: x: 2, y: 2, z: 4, core: 2. Of those that a mesh axis runs over, the one named last changes fastest.
Arguments:
- tokens: bfloat16 [4096, 2048], P(('expert', 'dp')), may hold values from -6 to 6
- cotangent: bfloat16 [4096, 2048], P(('expert', 'dp')), may hold values from -6 to 6
- gates: float32 [4096, 2], P(('expert', 'dp')), may hold values from 0.2 to 1
- expert_ids: int32 [4096, 2], P(('expert', 'dp')), may hold values from 0 to 7, all different within a row; in each aligned block of 128 rows (0 to 127, 128 to 255, ...) at most 40 rows name the same one
- w_in: bfloat16 [8, 2048, 704], P('expert'), may hold values from -0.125 to 0.125
- w_out: bfloat16 [8, 704, 2048], P('expert'), may hold values from -0.21875 to 0.21875
Outputs:
- grad_tokens: bfloat16 [4096, 2048], P(('expert', 'dp'))
- grad_w_out: bfloat16 [8, 704, 2048], P('expert', None, 'dp')
Inputs may be any that keep to these rules, and one draw needn't show every extreme that they name: `expert_ids`: the 2 ids of a token differ. In the rows of one device (aligned blocks of 128 rows), no expert is named more than 40 times.
All inputs are finite; a program needn't handle non-finite values.
Results may differ from a plain program's by a relative error of at most 0.018.
Values may be sent and summed in bfloat16 or wider, within the bound.
A program may use at most 64 MiB of HBM per device.

v0:
```python
import jax
import jax.numpy as jnp
from jax import lax
from jax.sharding import PartitionSpec as P


def per_device(tokens, cotangent, gates, expert_ids, w_in, w_out):
    tok_rows, model_width = tokens.shape
    top_count = expert_ids.shape[1]
    experts = lax.axis_size("expert")
    capacity = 5 * tok_rows * top_count // (4 * experts)
    flat_ids = expert_ids.reshape(-1)
    assign_count = flat_ids.shape[0]
    onehot_table = (flat_ids[:, None] == jnp.arange(experts, dtype=jnp.int32)[None, :]).astype(
        jnp.int32
    )
    before = jnp.cumsum(onehot_table, axis=0) - onehot_table
    position = jnp.sum(before * onehot_table, axis=1)
    slot_of = flat_ids * capacity + position
    target = jnp.arange(experts * capacity, dtype=jnp.int32)
    matches = slot_of[None, :] == target[:, None]
    filled = jnp.any(matches, axis=1)
    owner_rows = jnp.arange(assign_count, dtype=jnp.int32) // top_count
    source = jnp.sum(jnp.where(matches, owner_rows[None, :], 0), axis=1)
    weight_slot = jnp.sum(jnp.where(matches, gates.reshape(-1)[None, :], jnp.float32(0.0)), axis=1)
    sent_rows = jnp.where(filled[:, None], tokens[source], jnp.zeros((), tokens.dtype))
    sent_grads = jnp.where(
        filled[:, None],
        cotangent[source].astype(jnp.float32) * weight_slot[:, None],
        jnp.float32(0.0),
    ).astype(jnp.bfloat16)
    got_rows, got_grads = (
        lax.all_to_all(
            sent_rows.reshape(experts, capacity, model_width),
            "expert",
            split_axis=0,
            concat_axis=0,
            tiled=True,
        ),
        lax.all_to_all(
            sent_grads.reshape(experts, capacity, model_width),
            "expert",
            split_axis=0,
            concat_axis=0,
            tiled=True,
        ),
    )
    got_rows = got_rows.reshape(-1, model_width)
    got_grads = got_grads.reshape(-1, model_width)
    w_first = w_in[0]
    w_second = w_out[0]
    dims_t = (((1,), (1,)), ((), ()))
    pre_act = jnp.dot(got_rows, w_first, preferred_element_type=jnp.float32)
    sigmoid_pre = jax.nn.sigmoid(pre_act)
    act = (pre_act * sigmoid_pre).astype(jnp.bfloat16)
    back_proj = lax.dot_general(got_grads, w_second, dims_t, preferred_element_type=jnp.float32)
    dpre_act = (back_proj * sigmoid_pre * (1.0 + pre_act * (1.0 - sigmoid_pre))).astype(
        jnp.bfloat16
    )
    grad_rows = lax.dot_general(
        dpre_act, w_first, dims_t, preferred_element_type=jnp.float32
    ).astype(jnp.bfloat16)
    returned = lax.all_to_all(
        grad_rows.reshape(experts, capacity, model_width),
        "expert",
        split_axis=0,
        concat_axis=0,
        tiled=True,
    ).reshape(-1, model_width)
    picked = returned[slot_of].astype(jnp.float32).reshape(tok_rows, top_count, model_width)
    grad_tokens = jnp.sum(picked, axis=1).astype(jnp.bfloat16)
    dims_rows = (((0,), (0,)), ((), ()))
    grad_share = lax.psum_scatter(
        lax.dot_general(got_grads, act, dims_rows, preferred_element_type=jnp.float32)
        .astype(jnp.bfloat16)
        .astype(jnp.float32)
        .astype(jnp.bfloat16),
        "dp",
        scatter_dimension=0,
        tiled=True,
    )
    grad_w_out = grad_share.T[None]
    return (grad_tokens, grad_w_out)


def solution(mesh):
    in_specs = (
        P(("expert", "dp"), None),
        P(("expert", "dp"), None),
        P(("expert", "dp"), None),
        P(("expert", "dp"), None),
        P("expert", None, None),
        P("expert", None, None),
    )
    out_specs = (P(("expert", "dp"), None), P("expert", None, "dp"))
    return jax.shard_map(
        per_device, mesh=mesh, in_specs=in_specs, out_specs=out_specs, check_vma=False
    )
```

profile of v0, /device:TPU:1, one launch (start us, length us, event | category | flops | bytes accessed | tf_op | source)
XLA Modules:
  0.0 159.4 jit_solution(10847163479395505315)
XLA Ops:
  7.2 0.0 copy-start
  7.2 0.9 copy.12
  8.1 0.1 reshape.123
  8.3 0.1 eq.39
  8.4 0.6 reduce-window.6
  9.0 0.2 slice_reduce_fusion
  9.3 0.1 fusion.26
  9.4 0.2 fusion.24
  9.5 0.1 broadcast_in_dim.63
  9.6 0.2 select_reduce_fusion.1
  9.8 6.1 %gather_fusion.1 = bf16[320,2048]{1,0:T(8,128)(2,1)} fusion(bf16[128,2048]{1,0:T(8,128)(2,1)} %param.6, s32[1024]{0:T(1024)S(1)} %pad_clamp_fusion.1), kind=kCustom, calls=%fused_computation.1 | custom fusion | bytes 2622720 | tf_op jit(solution)/shard_map/gather | solution.py:26
  15.9 2.6 %broadcast_select_fusion = bf16[8,40,2048]{2,1,0:T(8,128)(2,1)} fusion(bf16[8,40,2048]{2,1,0:T(8,128)(2,1)} %bitcast.42, pred[8,40]{1,0:T(8,128)(4,1)S(1)} %broadcast_in_dim.63), kind=kLoop, calls=%fused_computation.16 | loop fusion | flops 655360 | bytes 2621760 | tf_op jit(solution)/shard_map/jit(_where)/select_n | solution.py:26
  18.4 0.0 copy-start.3
  18.4 0.0 copy-start.1
  18.4 6.5 %all-to-all-start.1 = ((bf16[8,40,2048]{2,1,0:T(8,128)(2,1)}), bf16[8,40,2048]{2,1,0:T(8,128)(2,1)}, u32[]{:S(2)}, u32[]{:S(2)}) async-start(bf16[8,40,2048]{2,1,0:T(8,128)(2,1)} %broadcast_select_fusion), calls=%async_computation.1 | async-start | bytes 2621440 | tf_op jit(solution)/shard_map/all_to_all | solution.py:33
  25.0 0.0 copy-done.3
  25.0 0.1 copy.14
  25.1 0.1 broadcast_in_dim.67
  25.2 0.2 select_reduce_fusion
  25.4 0.1 mul.53
  25.4 0.0 copy-done.1
  25.4 3.0 %gather_fusion = bf16[320,2048]{1,0:T(8,128)(2,1)} fusion(bf16[128,2048]{1,0:T(8,128)(2,1)S(1)} %copy-done.1, s32[1024]{0:T(1024)S(1)} %pad_clamp_fusion.1), kind=kCustom, calls=%fused_computation | custom fusion | bytes 2622720 | tf_op jit(solution)/shard_map/gather | solution.py:29
  28.5 2.8 %fusion.10 = bf16[8,40,2048]{2,1,0:T(8,128)(2,1)} fusion(bf16[8,40,2048]{2,1,0:T(8,128)(2,1)} %bitcast.41, f32[8,40]{1,0:T(8,128)S(1)} %mul.53, pred[8,40]{1,0:T(8,128)(4,1)S(1)} %broadcast_in_dim.63), kind=kLoop, calls=%fused_computation.13 | loop fusion | flops 2621440 | bytes 2623040 | tf_op jit(solution)/shard_map/convert_element_type | solution.py:31
  31.3 25.2 %all-to-all-done.1 = bf16[8,40,2048]{2,1,0:T(8,128)(2,1)} async-done(((bf16[8,40,2048]{2,1,0:T(8,128)(2,1)}), bf16[8,40,2048]{2,1,0:T(8,128)(2,1)}, u32[]{:S(2)}, u32[]{:S(2)}) %all-to-all-start.1) | async-done | bytes 1310752 | tf_op jit(solution)/shard_map/all_to_all | solution.py:33
  56.4 5.0 %all-to-all-start = ((bf16[8,40,2048]{2,1,0:T(8,128)(2,1)}), bf16[8,40,2048]{2,1,0:T(8,128)(2,1)}, u32[]{:S(2)}, u32[]{:S(2)}) async-start(bf16[8,40,2048]{2,1,0:T(8,128)(2,1)} %fusion.10), calls=%async_computation | async-start | bytes 2621440 | tf_op jit(solution)/shard_map/all_to_all | solution.py:40
  61.4 0.0 reduce-scatter.2.cloned.1.call-start
  61.4 0.0 copy-done
  61.4 3.5 %fusion.2 = f32[320,704]{1,0:T(8,128)} fusion(bf16[320,2048]{1,0:T(8,128)(2,1)} %bitcast.6, bf16[1,2048,704]{1,2,0:T(8,128)(2,1)S(1)} %copy-done), kind=kOutput, calls=%fused_computation.6 | convolution fusion | flops 922746880 | bytes 5095424 | tf_op jit(solution)/shard_map/dot_general | solution.py:53
  64.9 27.9 %all-to-all-done = bf16[8,40,2048]{2,1,0:T(8,128)(2,1)} async-done(((bf16[8,40,2048]{2,1,0:T(8,128)(2,1)}), bf16[8,40,2048]{2,1,0:T(8,128)(2,1)}, u32[]{:S(2)}, u32[]{:S(2)}) %all-to-all-start) | async-done | bytes 1310752 | tf_op jit(solution)/shard_map/all_to_all | solution.py:40
  92.9 4.9 %convolution_convert_fusion = bf16[2048,704]{0,1:T(8,128)(2,1)} fusion(bf16[320,2048]{1,0:T(8,128)(2,1)} %bitcast.3, f32[320,704]{1,0:T(8,128)} %fusion.2), kind=kOutput, calls=%fused_computation.3 | convolution fusion | flops 925315072 | bytes 5095424 | tf_op jit(solution)/shard_map/dot_general | solution.py:74
  97.8 0.0 reduce-scatter.2.cloned.1.call-update
  97.8 6.2 %fusion.6 = bf16[320,2048]{1,0:T(8,128)(2,1)} fusion(bf16[1,2048,704]{1,2,0:T(8,128)(2,1)S(1)} %copy-done, bf16[320,2048]{1,0:T(8,128)(2,1)} %bitcast.3, bf16[1,704,2048]{2,1,0:T(8,128)(2,1)} %param.11, f32[320,704]{1,0:T(8,128)} %fusion.2), kind=kOutput, calls=%fused_computation.10 | convolution fusion | flops 1848176640 | bytes 9289728 | tf_op jit(solution)/shard_map/dot_general | solution.py:60
  104.0 0.0 copy-start.2
  104.0 5.1 %all-to-all-start.2 = ((bf16[8,40,2048]{2,1,0:T(8,128)(2,1)}), bf16[8,40,2048]{2,1,0:T(8,128)(2,1)}, u32[]{:S(2)}, u32[]{:S(2)}) async-start(bf16[8,40,2048]{2,1,0:T(8,128)(2,1)} %bitcast.43), calls=%async_computation.2 | async-start | bytes 2621440 | tf_op jit(solution)/shard_map/all_to_all | solution.py:63
  109.2 0.0 copy-done.2
  109.2 0.1 copy.15
  109.3 0.1 mul.61
  109.4 31.2 %all-to-all-done.2 = bf16[8,40,2048]{2,1,0:T(8,128)(2,1)} async-done(((bf16[8,40,2048]{2,1,0:T(8,128)(2,1)}), bf16[8,40,2048]{2,1,0:T(8,128)(2,1)}, u32[]{:S(2)}, u32[]{:S(2)}) %all-to-all-start.2) | async-done | bytes 1310752 | tf_op jit(solution)/shard_map/all_to_all | solution.py:63
  140.6 4.8 %gather_fusion.2 = bf16[256,2048]{1,0:T(8,128)(2,1)} fusion(bf16[320,2048]{1,0:T(8,128)(2,1)} %bitcast.9, s32[1024]{0:T(1024)S(1)} %pad_clamp_fusion), kind=kCustom, calls=%fused_computation.2 | custom fusion | bytes 2098176 | tf_op jit(solution)/shard_map/gather | solution.py:70
  145.5 2.5 %gather.17 = bf16[128,2,2048]{2,1,0:T(2,128)(2,1)} reshape(bf16[256,2048]{1,0:T(8,128)(2,1)} %gather_fusion.2) | data formatting | bytes 2097152 | tf_op jit(solution)/shard_map/gather | solution.py:70
  148.0 4.6 %reduce_sum.48 = bf16[128,2048]{1,0:T(8,128)(2,1)} reduce(bf16[128,2,2048]{2,1,0:T(2,128)(2,1)} %gather.17, bf16[]{:T(256)} %constant.36.clone.1), dimensions={1}, to_apply=%region_6.7 | reduce | flops 262144 | bytes 1572866 | tf_op jit(solution)/shard_map/reduce_sum | solution.py:71
  152.6 0.0 reduce-scatter.2.cloned.1.call-done
  (9 shorter events, 0.1 us)
Async XLA Ops:
  7.2 54.3 %copy-start = (bf16[1,2048,704]{1,2,0:T(8,128)(2,1)S(1)}, bf16[1,2048,704]{1,2,0:T(8,128)(2,1)}, u32[]{:S(2)}) copy-start(bf16[1,2048,704]{1,2,0:T(8,128)(2,1)} %param.10) | copy-start | bytes 8650756
  18.4 6.5 %copy-start.3 = (f32[128,2]{0,1:T(2,128)S(1)}, f32[128,2]{0,1:T(2,128)}, u32[]{:S(2)}) copy-start(f32[128,2]{0,1:T(2,128)} %param.8) | copy-start | bytes 3076
  18.4 7.0 %copy-start.1 = (bf16[128,2048]{1,0:T(8,128)(2,1)S(1)}, bf16[128,2048]{1,0:T(8,128)(2,1)}, u32[]{:S(2)}) copy-start(bf16[128,2048]{1,0:T(8,128)(2,1)} %param.7) | copy-start | bytes 1572868
  18.4 38.0 %all-to-all-start.1 = ((bf16[8,40,2048]{2,1,0:T(8,128)(2,1)}), bf16[8,40,2048]{2,1,0:T(8,128)(2,1)}, u32[]{:S(2)}, u32[]{:S(2)}) async-start(bf16[8,40,2048]{2,1,0:T(8,128)(2,1)} %broadcast_select_fusion), calls=%async_computation.1 | async-start | bytes 2621440 | tf_op jit(solution)/shard_map/all_to_all | solution.py:33
  56.4 36.5 %all-to-all-start = ((bf16[8,40,2048]{2,1,0:T(8,128)(2,1)}), bf16[8,40,2048]{2,1,0:T(8,128)(2,1)}, u32[]{:S(2)}, u32[]{:S(2)}) async-start(bf16[8,40,2048]{2,1,0:T(8,128)(2,1)} %fusion.10), calls=%async_computation | async-start | bytes 2621440 | tf_op jit(solution)/shard_map/all_to_all | solution.py:40
  61.4 91.1 %reduce-scatter.2.cloned.1.call-start = ((), (), s32[]{:S(2)}) async-start(), calls=%async_computation.4 | async-start | bytes 3604480 | tf_op jit(solution)/shard_map/reduce_scatter | solution.py:73
  104.0 5.1 %copy-start.2 = (s32[128,2]{0,1:T(2,128)S(1)}, s32[128,2]{0,1:T(2,128)}, u32[]{:S(2)}) copy-start(s32[128,2]{0,1:T(2,128)} %param.9) | copy-start | bytes 3076
  104.0 36.6 %all-to-all-start.2 = ((bf16[8,40,2048]{2,1,0:T(8,128)(2,1)}), bf16[8,40,2048]{2,1,0:T(8,128)(2,1)}, u32[]{:S(2)}, u32[]{:S(2)}) async-start(bf16[8,40,2048]{2,1,0:T(8,128)(2,1)} %bitcast.43), calls=%async_computation.2 | async-start | bytes 2621440 | tf_op jit(solution)/shard_map/all_to_all | solution.py:63
Sparse Core Ops, SparseCore 0:
  98.0 40.8 reduce-scatter.1
where the time goes:
time: 161 us; the launch traced here: 159 us
  waiting for transfers between devices  84.3 us (52%)
  local copies, waits for them, and re-layouts  18.6 us (12%)
  starting transfers between devices  16.7 us (10%)
  matrix products  14.6 us (9%)
  between operations  14.1 us (9%)
  other arithmetic  11.1 us (7%)
    all_to_all x1, waiting for transfers between devices, per_device(): lax.all_to_all(grad_rows.reshape(experts, capacity, model_width), 'expert...  31.2 us
    all_to_all x1, waiting for transfers between devices, per_device(): lax.all_to_all(sent_grads.reshape(experts, capacity, model_width), 'exper...  27.9 us
    all_to_all x1, waiting for transfers between devices, per_device(): lax.all_to_all(sent_rows.reshape(experts, capacity, model_width), 'expert...  25.2 us
    gather x2, local copies, waits for them, and re-layouts, per_device(): returned[slot_of].astype(jnp.float32)  7.36 us
    all_to_all x1, starting transfers between devices, per_device(): lax.all_to_all(sent_rows.reshape(experts, capacity, model_width), 'expert...  6.51 us
    dot_general x1, matrix products, per_device(): lax.dot_general(dpre_act, w_first, dims_t, preferred_element_type=jnp.flo...  6.17 us
    gather x1, local copies, waits for them, and re-layouts, per_device(): tokens[source]  6.09 us
    all_to_all x1, starting transfers between devices, per_device(): lax.all_to_all(grad_rows.reshape(experts, capacity, model_width), 'expert...  5.14 us
  transfers between devices with their start and end apart: 4, of which 3 were waited for; matrix products, arithmetic and copies ran while one was open for 18% of the time, Pallas kernels for 0%

commit v1 on v0

v1 whole, which is shorter than its diff:
```python
import functools

import jax
import jax.numpy as jnp
from jax import lax
from jax.experimental import pallas as pl
from jax.experimental.pallas import tpu as pltpu
from jax.sharding import PartitionSpec as P

BY_COLS = (((1,), (1,)), ((), ()))
BY_ROWS = (((0,), (0,)), ((), ()))


def layer_kernel(
    experts, groups, tokens, cotangent, gates, ids, w_in_hbm, w_out_hbm, grad_tokens, grad_w,
    w_in, w_out, places, gains, sent_rows, sent_grads, got_rows, got_grads, dpre, sent_back,
    got_back, total, w_total, w_sent, w_got, load_sems, send_sems, recv_sems, w_send, w_recv,
):
    me = lax.axis_index("expert")
    group = lax.axis_index("dp")
    half = experts // 2
    slots = got_rows.shape[1]
    columns = grad_w.shape[1]

    loads = [
        pltpu.make_async_copy(w_in_hbm, w_in, load_sems.at[0]),
        pltpu.make_async_copy(w_out_hbm, w_out, load_sems.at[1]),
    ]
    for load in loads:
        load.start()

    barrier = pltpu.get_barrier_semaphore()

    def greet_expert(step, carry):
        pl.semaphore_signal(barrier, inc=1, device_id={"expert": (me + step) % experts})
        return carry

    def greet_group(step, carry):
        pl.semaphore_signal(barrier, inc=1, device_id={"dp": (group + step) % groups})
        return carry

    lax.fori_loop(1, experts, greet_expert, 0)
    lax.fori_loop(1, groups, greet_group, 0)

    my_half = me // half
    other = (1 - my_half) * half

    def target(step):
        return jnp.where(
            step < half, other + (me + step) % half, my_half * half + (me + step - half + 1) % half
        )

    def origin(step):
        return jnp.where(
            step < half,
            other + (me + half - step % half) % half,
            my_half * half + (me + 2 * half - step % half - 1) % half,
        )

    def exchange(kind, source, dest, peer, here, there):
        return pltpu.make_async_remote_copy(
            src_ref=source.at[here],
            dst_ref=dest.at[there],
            send_sem=send_sems.at[kind, here],
            recv_sem=recv_sems.at[kind, there],
            device_id={"expert": peer},
        )

    rows = tokens.shape[0]
    expert_of = lax.broadcasted_iota(jnp.int32, (experts, rows), 0)
    chosen = jnp.zeros((experts, rows), jnp.float32)
    gain = jnp.zeros((experts, rows), jnp.float32)
    for k in range(ids.shape[0]):
        hit = expert_of == ids[k : k + 1, :]
        chosen = chosen + jnp.where(hit, 1.0, 0.0)
        gain = gain + jnp.where(hit, gates[k : k + 1, :], 0.0)
    earlier = jnp.where(
        lax.broadcasted_iota(jnp.int32, (rows, rows), 0)
        < lax.broadcasted_iota(jnp.int32, (rows, rows), 1),
        1.0,
        0.0,
    ).astype(jnp.bfloat16)
    place = jnp.dot(chosen.astype(jnp.bfloat16), earlier, preferred_element_type=jnp.float32)
    places[...] = jnp.where(chosen > 0.0, place, -1.0)
    gains[...] = gain
    slot_number = lax.broadcasted_iota(jnp.int32, (slots, rows), 0).astype(jnp.float32)

    def choose(expert):
        return slot_number == places[pl.ds(expert, 1), :]

    def pack(expert, rows_to, grads_to):
        match = choose(expert)
        pick = jnp.where(match, 1.0, 0.0).astype(jnp.bfloat16)
        weight = jnp.sum(jnp.where(match, gains[pl.ds(expert, 1), :], 0.0), axis=1, keepdims=True)
        picked = jnp.dot(pick, tokens[...], preferred_element_type=jnp.float32)
        rows_to[expert] = picked.astype(jnp.bfloat16)
        gated = jnp.dot(pick, cotangent[...], preferred_element_type=jnp.float32) * weight
        grads_to[expert] = gated.astype(jnp.bfloat16)

    pl.semaphore_wait(barrier, experts + groups - 2)

    def dispatch(step, carry):
        to = target(step)
        pack(to, sent_rows, sent_grads)
        exchange(0, sent_rows, got_rows, to, to, me).start()
        exchange(1, sent_grads, got_grads, to, to, me).start()
        return carry

    lax.fori_loop(0, experts - 1, dispatch, 0)
    pack(me, got_rows, got_grads)
    w_total[...] = jnp.zeros_like(w_total)
    for load in loads:
        load.wait()

    def absorb(source):
        x = got_rows[source]
        dy = got_grads[source]
        pre = lax.dot_general(x, w_in[...], BY_COLS, preferred_element_type=jnp.float32)
        sig = 1.0 / (1.0 + jnp.exp(-pre))
        act = (pre * sig).astype(jnp.bfloat16)
        for g in range(groups):
            w_total[g] += lax.dot_general(
                act,
                dy[:, g * columns : (g + 1) * columns],
                BY_ROWS,
                preferred_element_type=jnp.float32,
            )
        back = lax.dot_general(dy, w_out[...], BY_COLS, preferred_element_type=jnp.float32)
        dpre[source] = (back * sig * (1.0 + pre * (1.0 - sig))).astype(jnp.bfloat16)

    absorb(me)

    def receive(step, carry):
        source = origin(step)
        exchange(0, sent_rows, got_rows, source, source, source).wait_recv()
        exchange(1, sent_grads, got_grads, source, source, source).wait_recv()
        absorb(source)
        return carry

    lax.fori_loop(0, experts - 1, receive, 0)

    def share(to, slot):
        return pltpu.make_async_remote_copy(
            src_ref=w_sent.at[to],
            dst_ref=w_got.at[slot],
            send_sem=w_send.at[to],
            recv_sem=w_recv.at[slot],
            device_id={"dp": to},
        )

    def spread(step, carry):
        to = (group + step) % groups
        w_sent[to] = w_total[to].astype(jnp.bfloat16)
        share(to, group).start()
        return carry

    lax.fori_loop(1, groups, spread, 0)

    def rows_of(source):
        return jnp.dot(dpre[source], w_in[...], preferred_element_type=jnp.float32).astype(
            jnp.bfloat16
        )

    def give_back(step, carry):
        to = target(step)
        sent_back[to] = rows_of(to)
        exchange(2, sent_back, got_back, to, to, me).start()
        return carry

    lax.fori_loop(0, experts - 1, give_back, 0)
    got_back[me] = rows_of(me)

    def combine(source):
        pick = jnp.where(choose(source), 1.0, 0.0).astype(jnp.bfloat16)
        return lax.dot_general(pick, got_back[source], BY_ROWS, preferred_element_type=jnp.float32)

    total[...] = combine(me)

    def take_back(step, carry):
        source = origin(step)
        exchange(2, sent_back, got_back, source, source, source).wait_recv()
        total[...] += combine(source)
        return carry

    lax.fori_loop(0, experts - 1, take_back, 0)
    grad_tokens[...] = total[...].astype(jnp.bfloat16)

    w_total[group] = w_total[group].astype(jnp.bfloat16).astype(jnp.float32)

    def gather(step, carry):
        source = (group + step) % groups
        share(source, source).wait_recv()
        w_total[group] += w_got[source].astype(jnp.float32)
        return carry

    lax.fori_loop(1, groups, gather, 0)
    grad_w[...] = w_total[group].astype(jnp.bfloat16)

    def drain(step, carry):
        to = target(step)
        exchange(0, sent_rows, got_rows, to, to, me).wait_send()
        exchange(1, sent_grads, got_grads, to, to, me).wait_send()
        exchange(2, sent_back, got_back, to, to, me).wait_send()
        return carry

    def drain_group(step, carry):
        share((group + step) % groups, group).wait_send()
        return carry

    lax.fori_loop(0, experts - 1, drain, 0)
    lax.fori_loop(1, groups, drain_group, 0)


def per_device(tokens, cotangent, gates, expert_ids, w_in, w_out):
    rows, width = tokens.shape
    hidden = w_out.shape[1]
    experts, groups = lax.axis_size("expert"), lax.axis_size("dp")
    capacity = 5 * rows * expert_ids.shape[1] // (4 * experts)
    slots = -(-capacity // 8) * 8
    columns = width // groups
    blocks = pltpu.VMEM((experts, slots, width), jnp.bfloat16)
    shares = pltpu.VMEM((groups, hidden, columns), jnp.bfloat16)
    vmem = pl.BlockSpec(memory_space=pltpu.VMEM)
    anywhere = pl.BlockSpec(memory_space=pl.ANY)
    multiplies = experts * slots * width * hidden
    grad_tokens, grad_w = pl.pallas_call(
        functools.partial(layer_kernel, experts, groups),
        out_shape=(
            jax.ShapeDtypeStruct((rows, width), jnp.bfloat16),
            jax.ShapeDtypeStruct((hidden, columns), jnp.bfloat16),
        ),
        in_specs=[vmem] * 4 + [anywhere] * 2,
        out_specs=(vmem, vmem),
        scratch_shapes=[
            pltpu.VMEM((hidden, width), jnp.bfloat16),
            pltpu.VMEM((hidden, width), jnp.bfloat16),
            pltpu.VMEM((experts, rows), jnp.float32),
            pltpu.VMEM((experts, rows), jnp.float32),
            blocks,
            blocks,
            blocks,
            blocks,
            pltpu.VMEM((experts, slots, hidden), jnp.bfloat16),
            blocks,
            blocks,
            pltpu.VMEM((rows, width), jnp.float32),
            pltpu.VMEM((groups, hidden, columns), jnp.float32),
            shares,
            shares,
            pltpu.SemaphoreType.DMA((2,)),
            pltpu.SemaphoreType.DMA((3, experts)),
            pltpu.SemaphoreType.DMA((3, experts)),
            pltpu.SemaphoreType.DMA((groups,)),
            pltpu.SemaphoreType.DMA((groups,)),
        ],
        compiler_params=pltpu.CompilerParams(
            collective_id=0, has_side_effects=True, vmem_limit_bytes=56 * 1024 * 1024
        ),
        cost_estimate=pl.CostEstimate(
            flops=8 * multiplies, bytes_accessed=4 * hidden * width, transcendentals=0
        ),
    )(
        tokens,
        cotangent,
        gates.T,
        expert_ids.T,
        jnp.swapaxes(w_in[0], 0, 1),
        w_out[0],
    )
    return grad_tokens, grad_w[None]


def solution(mesh):
    split = P(("expert", "dp"), None)
    whole = P("expert", None, None)
    return jax.shard_map(
        per_device,
        mesh=mesh,
        in_specs=(split, split, split, split, whole, whole),
        out_specs=(split, P("expert", None, "dp")),
        check_vma=False,
    )
```

time: 161 us -> 111 us (0.69)
  the two profiles are of different devices: /device:TPU:1 before, /device:TPU:19 now
where the time goes in v1:
time: 111 us
  Pallas kernels  106 us (95%)
  local copies, waits for them, and re-layouts  3.89 us (4%)
    pallas_call x1, Pallas kernels, per_device(): pl.pallas_call(functools.partial(layer_kernel, experts, groups), out_shap...  106 us
    unnamed x2, local copies, waits for them, and re-layouts  3.89 us

profile of v1, /device:TPU:19, one launch (start us, length us, event | category | flops | bytes accessed | tf_op | source)
XLA Modules:
  0.0 110.7 jit_solution(16405164156327765131)
XLA Ops:
  0.6 106.1 %shard_map.77 = (bf16[128,2048]{1,0:T(8,128)(2,1)}, bf16[704,512]{1,0:T(8,128)(2,1)}) custom-call(bf16[128,2048]{1,0:T(8,128)(2,1)} %tokens.1, bf16[128,2048]{1,0:T(8,128)(2,1)} %cotangent.1, f32[2,128]{1,0:T(2,128)} %bitcast.10, s32[2,128]{1,0:T(2,128)} %bitcast.11, bf16[704,2048]{1,0:T(8,128)(2,1)} %bitcast.8, bf16[704,2048]{1,0:T(8,128)(2,1)} %bitcast.9), custom_call_target="tpu_custom_call" | custom-call | flops 3690987520 | bytes 5767168 | tf_op jit(solution)/shard_map/pallas_call | solution.py:226
  106.8 1.9 %copy.10 = bf16[128,2048]{1,0:T(8,128)(2,1)} copy(bf16[128,2048]{1,0:T(8,128)(2,1)} %get-tuple-element.8) | data formatting | bytes 1048576
  108.6 2.0 %copy.11 = bf16[1,704,512]{2,1,0:T(8,128)(2,1)} copy(bf16[1,704,512]{2,1,0:T(8,128)(2,1)} %bitcast.7) | data formatting | bytes 1441792

commit v2 on v1

v2 whole, which is shorter than its diff:
```python
import functools

import jax
import jax.numpy as jnp
from jax import lax
from jax.experimental import pallas as pl
from jax.experimental.pallas import tpu as pltpu
from jax.sharding import PartitionSpec as P

BY_COLS = (((1,), (1,)), ((), ()))
BY_ROWS = (((0,), (0,)), ((), ()))


def layer_kernel(
    experts, groups, pieces, tokens, cotangent, gates, ids, w_in_hbm, w_out_hbm, grad_tokens,
    grad_w, w_in, w_out, places, gains, sent_rows, sent_grads, got_rows, got_grads, act, slope,
    back, sent_back, got_back, total, w_own, w_sent, w_got, load_sems, row_send, row_recv,
    grad_send, grad_recv, back_send, back_recv, w_send, w_recv,
):
    me = lax.axis_index("expert")
    group = lax.axis_index("dp")
    half = experts // 2
    slots = got_rows.shape[1]
    columns = grad_w.shape[1]
    per_piece = groups // pieces
    width = per_piece * columns
    my_piece = group // per_piece

    loads = [pltpu.make_async_copy(w_in_hbm, w_in, load_sems.at[pieces])] + [
        pltpu.make_async_copy(
            w_out_hbm.at[:, pl.ds(p * width, width)], w_out.at[p], load_sems.at[p]
        )
        for p in range(pieces)
    ]
    for load in loads:
        load.start()

    barrier = pltpu.get_barrier_semaphore()

    def greet_expert(step, carry):
        pl.semaphore_signal(barrier, inc=1, device_id={"expert": (me + step) % experts})
        return carry

    def greet_group(step, carry):
        pl.semaphore_signal(barrier, inc=1, device_id={"dp": (group + step) % groups})
        return carry

    lax.fori_loop(1, experts, greet_expert, 0)
    lax.fori_loop(1, groups, greet_group, 0)

    my_half = me // half
    other = (1 - my_half) * half

    def target(step):
        return jnp.where(
            step < half, other + (me + step) % half, my_half * half + (me + step - half + 1) % half
        )

    def origin(step):
        return jnp.where(
            step < half,
            other + (me + half - step % half) % half,
            my_half * half + (me + 2 * half - step % half - 1) % half,
        )

    def piece_of(turn):
        return (my_piece + 1 + turn) % pieces

    def rows_copy(to, here, there):
        return pltpu.make_async_remote_copy(
            src_ref=sent_rows.at[here],
            dst_ref=got_rows.at[there],
            send_sem=row_send.at[here],
            recv_sem=row_recv.at[there],
            device_id={"expert": to},
        )

    def grads_copy(piece, to, here, there):
        return pltpu.make_async_remote_copy(
            src_ref=sent_grads.at[piece, here],
            dst_ref=got_grads.at[piece, there],
            send_sem=grad_send.at[piece, here],
            recv_sem=grad_recv.at[piece, there],
            device_id={"expert": to},
        )

    def back_copy(to, here, there):
        return pltpu.make_async_remote_copy(
            src_ref=sent_back.at[here],
            dst_ref=got_back.at[there],
            send_sem=back_send.at[here],
            recv_sem=back_recv.at[there],
            device_id={"expert": to},
        )

    rows = tokens.shape[0]
    expert_of = lax.broadcasted_iota(jnp.int32, (experts, rows), 0)
    chosen = jnp.zeros((experts, rows), jnp.float32)
    gain = jnp.zeros((experts, rows), jnp.float32)
    for k in range(ids.shape[0]):
        hit = expert_of == ids[k : k + 1, :]
        chosen = chosen + jnp.where(hit, 1.0, 0.0)
        gain = gain + jnp.where(hit, gates[k : k + 1, :], 0.0)
    earlier = jnp.where(
        lax.broadcasted_iota(jnp.int32, (rows, rows), 0)
        < lax.broadcasted_iota(jnp.int32, (rows, rows), 1),
        1.0,
        0.0,
    ).astype(jnp.bfloat16)
    place = jnp.dot(chosen.astype(jnp.bfloat16), earlier, preferred_element_type=jnp.float32)
    places[...] = jnp.where(chosen > 0.0, place, -1.0)
    gains[...] = gain
    slot_number = lax.broadcasted_iota(jnp.int32, (slots, rows), 0).astype(jnp.float32)

    def choose(expert):
        return slot_number == places[pl.ds(expert, 1), :]

    def pack_rows(expert, into):
        pick = jnp.where(choose(expert), 1.0, 0.0).astype(jnp.bfloat16)
        picked = jnp.dot(pick, tokens[...], preferred_element_type=jnp.float32)
        into[expert] = picked.astype(jnp.bfloat16)

    def pack_grads(piece, expert, into):
        match = choose(expert)
        pick = jnp.where(match, 1.0, 0.0).astype(jnp.bfloat16)
        weight = jnp.sum(jnp.where(match, gains[pl.ds(expert, 1), :], 0.0), axis=1, keepdims=True)
        part = cotangent[:, pl.ds(pl.multiple_of(piece * width, width), width)]
        gated = jnp.dot(pick, part, preferred_element_type=jnp.float32) * weight
        into[piece, expert] = gated.astype(jnp.bfloat16)

    pl.semaphore_wait(barrier, experts + groups - 2)

    def send_rows(step, carry):
        to = target(step)
        pack_rows(to, sent_rows)
        rows_copy(to, to, me).start()
        return carry

    def send_grads(turn, step):
        to = target(step)
        piece = piece_of(turn)
        pack_grads(piece, to, sent_grads)
        grads_copy(piece, to, to, me).start()

    def send_first_grads(step, carry):
        send_grads(0, step)
        return carry

    lax.fori_loop(0, experts - 1, send_rows, 0)
    lax.fori_loop(0, experts - 1, send_first_grads, 0)
    pack_rows(me, got_rows)
    for p in range(pieces):
        pack_grads(p, me, got_grads)
    for load in loads:
        load.wait()

    def absorb_rows(source):
        pre = lax.dot_general(
            got_rows[source], w_in[...], BY_COLS, preferred_element_type=jnp.float32
        )
        sig = 1.0 / (1.0 + jnp.exp(-pre))
        act[source] = (pre * sig).astype(jnp.bfloat16)
        slope[source] = sig * (1.0 + pre * (1.0 - sig))

    def take_rows(step, carry):
        source = origin(step)
        rows_copy(source, source, source).wait_recv()
        absorb_rows(source)
        if pieces > 1:
            send_grads(1, step)
        return carry

    absorb_rows(me)
    lax.fori_loop(0, experts - 1, take_rows, 0)

    def back_part(piece, source):
        return lax.dot_general(
            got_grads[piece, source], w_out[piece], BY_COLS, preferred_element_type=jnp.float32
        )

    def give_back(source, into, done):
        dpre = (done * slope[source]).astype(jnp.bfloat16)
        into[source] = jnp.dot(dpre, w_in[...], preferred_element_type=jnp.float32).astype(
            jnp.bfloat16
        )

    def share(to, slot):
        return pltpu.make_async_remote_copy(
            src_ref=w_sent.at[to],
            dst_ref=w_got.at[slot],
            send_sem=w_send.at[to],
            recv_sem=w_recv.at[slot],
            device_id={"dp": to},
        )

    for turn in range(pieces):
        piece = piece_of(turn)
        last = turn == pieces - 1

        def take_grads(step, carry):
            source = origin(step)
            grads_copy(piece, source, source, source).wait_recv()
            done = back_part(piece, source)
            if turn > 0:
                done = done + back[source]
            if last:
                give_back(source, sent_back, done)
                back_copy(source, source, me).start()
            else:
                back[source] = done
            if turn + 2 < pieces:
                send_grads(turn + 2, step)
            return carry

        lax.fori_loop(0, experts - 1, take_grads, 0)
        mine = back_part(piece, me)
        if turn > 0:
            mine = mine + back[me]
        if last:
            give_back(me, got_back, mine)
        else:
            back[me] = mine
        down = lax.dot_general(
            act[...].reshape(experts * slots, act.shape[2]),
            got_grads[piece].reshape(experts * slots, width),
            BY_ROWS,
            preferred_element_type=jnp.float32,
        ).astype(jnp.bfloat16)
        for u in range(per_piece):
            to = piece * per_piece + u
            w_sent[to] = down[:, u * columns : (u + 1) * columns]
            if not last:
                share(to, group).start()
            elif per_piece > 1:
                pl.when(to != group)(lambda: share(to, group).start())

    def combine(source):
        pick = jnp.where(choose(source), 1.0, 0.0).astype(jnp.bfloat16)
        return lax.dot_general(pick, got_back[source], BY_ROWS, preferred_element_type=jnp.float32)

    total[...] = combine(me)

    w_own[...] = w_sent[group].astype(jnp.float32)

    def gather(step, carry):
        source = (group + step) % groups
        share(source, source).wait_recv()
        w_own[...] += w_got[source].astype(jnp.float32)
        return carry

    lax.fori_loop(1, groups, gather, 0)
    grad_w[...] = w_own[...].astype(jnp.bfloat16)

    def take_back(step, carry):
        source = target(step)
        back_copy(source, source, source).wait_recv()
        total[...] += combine(source)
        return carry

    lax.fori_loop(0, experts - 1, take_back, 0)
    grad_tokens[...] = total[...].astype(jnp.bfloat16)

    def drain(step, carry):
        to = target(step)
        rows_copy(to, to, me).wait_send()
        for p in range(pieces):
            grads_copy(p, to, to, me).wait_send()
        back_copy(to, to, me).wait_send()
        return carry

    def drain_group(step, carry):
        share((group + step) % groups, group).wait_send()
        return carry

    lax.fori_loop(0, experts - 1, drain, 0)
    lax.fori_loop(1, groups, drain_group, 0)


def hand_over(first, second, first_out, second_out, sems):
    copies = [
        pltpu.make_async_copy(first, first_out, sems.at[0]),
        pltpu.make_async_copy(second, second_out, sems.at[1]),
    ]
    for copy in copies:
        copy.start()
    for copy in copies:
        copy.wait()


def per_device(tokens, cotangent, gates, expert_ids, w_in, w_out):
    rows, width = tokens.shape
    hidden = w_out.shape[1]
    experts, groups = lax.axis_size("expert"), lax.axis_size("dp")
    capacity = 5 * rows * expert_ids.shape[1] // (4 * experts)
    slots = -(-capacity // 8) * 8
    columns = width // groups
    pieces = 4 if groups % 4 == 0 else 1
    blocks = pltpu.VMEM((experts, slots, width), jnp.bfloat16)
    parts = pltpu.VMEM((pieces, experts, slots, width // pieces), jnp.bfloat16)
    shares = pltpu.VMEM((groups, hidden, columns), jnp.bfloat16)
    vmem = pl.BlockSpec(memory_space=pltpu.VMEM)
    anywhere = pl.BlockSpec(memory_space=pl.ANY)
    multiplies = experts * slots * width * hidden
    outs = (
        jax.ShapeDtypeStruct((rows, width), jnp.bfloat16),
        jax.ShapeDtypeStruct((hidden, columns), jnp.bfloat16),
    )
    results = pl.pallas_call(
        functools.partial(layer_kernel, experts, groups, pieces),
        out_shape=outs,
        in_specs=[vmem] * 4 + [anywhere] * 2,
        out_specs=(vmem, vmem),
        scratch_shapes=[
            pltpu.VMEM((hidden, width), jnp.bfloat16),
            pltpu.VMEM((pieces, hidden, width // pieces), jnp.bfloat16),
            pltpu.VMEM((experts, rows), jnp.float32),
            pltpu.VMEM((experts, rows), jnp.float32),
            blocks,
            parts,
            blocks,
            parts,
            pltpu.VMEM((experts, slots, hidden), jnp.bfloat16),
            pltpu.VMEM((experts, slots, hidden), jnp.float32),
            pltpu.VMEM((experts, slots, hidden), jnp.float32),
            blocks,
            blocks,
            pltpu.VMEM((rows, width), jnp.float32),
            pltpu.VMEM((hidden, columns), jnp.float32),
            shares,
            shares,
            pltpu.SemaphoreType.DMA((pieces + 1,)),
            pltpu.SemaphoreType.DMA((experts,)),
            pltpu.SemaphoreType.DMA((experts,)),
            pltpu.SemaphoreType.DMA((pieces, experts)),
            pltpu.SemaphoreType.DMA((pieces, experts)),
            pltpu.SemaphoreType.DMA((experts,)),
            pltpu.SemaphoreType.DMA((experts,)),
            pltpu.SemaphoreType.DMA((groups,)),
            pltpu.SemaphoreType.DMA((groups,)),
        ],
        compiler_params=pltpu.CompilerParams(
            collective_id=0, has_side_effects=True, vmem_limit_bytes=56 * 1024 * 1024
        ),
        cost_estimate=pl.CostEstimate(
            flops=8 * multiplies, bytes_accessed=4 * hidden * width, transcendentals=0
        ),
    )(
        tokens,
        cotangent,
        gates.T,
        expert_ids.T,
        jnp.swapaxes(w_in[0], 0, 1),
        w_out[0],
    )
    grad_tokens, grad_w = pl.pallas_call(
        hand_over,
        out_shape=outs,
        in_specs=[anywhere] * 2,
        out_specs=(anywhere, anywhere),
        scratch_shapes=[pltpu.SemaphoreType.DMA((2,))],
        compiler_params=pltpu.CompilerParams(vmem_limit_bytes=56 * 1024 * 1024),
    )(*results)
    return grad_tokens, grad_w[None]


def solution(mesh):
    split = P(("expert", "dp"), None)
    whole = P("expert", None, None)
    return jax.shard_map(
        per_device,
        mesh=mesh,
        in_specs=(split, split, split, split, whole, whole),
        out_specs=(split, P("expert", None, "dp")),
        check_vma=False,
    )
```

time: 111 us -> 137 us (1.23)
  the two profiles are of different devices: /device:TPU:19 before, /device:TPU:1 now
where the time goes in v2:
time: 137 us
  Pallas kernels  136 us (99%)
    pallas_call x1, Pallas kernels, per_device(): pl.pallas_call(functools.partial(layer_kernel, experts, groups, pieces),...  97.5 us
    pallas_call x1, Pallas kernels, per_device(): pl.pallas_call(hand_over, out_shape=outs, in_specs=[anywhere] * 2, out_sp...  38.8 us

profile of v2, /device:TPU:1, one launch (start us, length us, event | category | flops | bytes accessed | tf_op | source)
XLA Modules:
  0.0 137.0 jit_solution(8989293890382759095)
XLA Ops:
  0.6 97.5 %shard_map.77 = (bf16[128,2048]{1,0:T(8,128)(2,1)}, bf16[704,512]{1,0:T(8,128)(2,1)}) custom-call(bf16[128,2048]{1,0:T(8,128)(2,1)} %tokens.1, bf16[128,2048]{1,0:T(8,128)(2,1)} %cotangent.1, f32[2,128]{1,0:T(2,128)} %bitcast.10, s32[2,128]{1,0:T(2,128)} %bitcast.11, bf16[704,2048]{1,0:T(8,128)(2,1)} %bitcast.7, bf16[704,2048]{1,0:T(8,128)(2,1)} %bitcast.8), custom_call_target="tpu_custom_call" | custom-call | flops 3690987520 | bytes 5767168 | tf_op jit(solution)/shard_map/pallas_call | solution.py:308
  98.2 38.8 %shard_map.78 = (bf16[128,2048]{1,0:T(8,128)(2,1)}, bf16[704,512]{1,0:T(8,128)(2,1)}) custom-call(bf16[128,2048]{1,0:T(8,128)(2,1)} %get-tuple-element.6.first, bf16[704,512]{1,0:T(8,128)(2,1)} %get-tuple-element.7.second), custom_call_target="tpu_custom_call" | custom-call | tf_op jit(solution)/shard_map/pallas_call | solution.py:355

commit v3 on v2

--- a/solution.py
+++ b/solution.py
@@ -276,15 +276,25 @@
     lax.fori_loop(1, groups, drain_group, 0)
 
 
-def hand_over(first, second, first_out, second_out, sems):
-    copies = [
-        pltpu.make_async_copy(first, first_out, sems.at[0]),
-        pltpu.make_async_copy(second, second_out, sems.at[1]),
-    ]
-    for copy in copies:
-        copy.start()
-    for copy in copies:
-        copy.wait()
+def hand_over(first, second, first_out, second_out, first_held, second_held, sems):
+    steps = []
+    for ref, held, out, which in (
+        (first, first_held, first_out, 0),
+        (second, second_held, second_out, 1),
+    ):
+        steps.append(
+            (
+                pltpu.make_async_copy(ref, held, sems.at[0, which]),
+                pltpu.make_async_copy(held, out, sems.at[1, which]),
+            )
+        )
+    for load, _ in steps:
+        load.start()
+    for load, store in steps:
+        load.wait()
+        store.start()
+    for _, store in steps:
+        store.wait()
 
 
 def per_device(tokens, cotangent, gates, expert_ids, w_in, w_out):
@@ -357,7 +367,11 @@
         out_shape=outs,
         in_specs=[anywhere] * 2,
         out_specs=(anywhere, anywhere),
-        scratch_shapes=[pltpu.SemaphoreType.DMA((2,))],
+        scratch_shapes=[
+            pltpu.VMEM(outs[0].shape, jnp.bfloat16),
+            pltpu.VMEM(outs[1].shape, jnp.bfloat16),
+            pltpu.SemaphoreType.DMA((2, 2)),
+        ],
         compiler_params=pltpu.CompilerParams(vmem_limit_bytes=56 * 1024 * 1024),
     )(*results)
     return grad_tokens, grad_w[None]

time: 137 us -> 101 us (0.74)
  Pallas kernels: 136 us -> 99.7 us
    pallas_call x1, Pallas kernels: 38.8 us -> 2.16 us  [per_device(): pl.pallas_call(hand_over, out_shape=outs, in_specs=[anywhere] * 2, out_sp...]
where the time goes in v3:
time: 101 us; the launch traced here: 100 us
  Pallas kernels  99.7 us (99%)
    pallas_call x1, Pallas kernels, per_device(): pl.pallas_call(functools.partial(layer_kernel, experts, groups, pieces),...  97.5 us
    pallas_call x1, Pallas kernels, per_device(): pl.pallas_call(hand_over, out_shape=outs, in_specs=[anywhere] * 2, out_sp...  2.16 us

profile of v3, /device:TPU:1, one launch (start us, length us, event | category | flops | bytes accessed | tf_op | source)
XLA Modules:
  0.0 100.3 jit_solution(13614837296775075959)
XLA Ops:
  0.6 97.5 %shard_map.77 = (bf16[128,2048]{1,0:T(8,128)(2,1)}, bf16[704,512]{1,0:T(8,128)(2,1)}) custom-call(bf16[128,2048]{1,0:T(8,128)(2,1)} %tokens.1, bf16[128,2048]{1,0:T(8,128)(2,1)} %cotangent.1, f32[2,128]{1,0:T(2,128)} %bitcast.10, s32[2,128]{1,0:T(2,128)} %bitcast.11, bf16[704,2048]{1,0:T(8,128)(2,1)} %bitcast.7, bf16[704,2048]{1,0:T(8,128)(2,1)} %bitcast.8), custom_call_target="tpu_custom_call" | custom-call | flops 3690987520 | bytes 5767168 | tf_op jit(solution)/shard_map/pallas_call | solution.py:318
  98.2 2.2 %shard_map.78 = (bf16[128,2048]{1,0:T(8,128)(2,1)}, bf16[704,512]{1,0:T(8,128)(2,1)}) custom-call(bf16[128,2048]{1,0:T(8,128)(2,1)} %get-tuple-element.6.first, bf16[704,512]{1,0:T(8,128)(2,1)} %get-tuple-element.7.second), custom_call_target="tpu_custom_call" | custom-call | tf_op jit(solution)/shard_map/pallas_call | solution.py:365

commit v4 on v3

v4 whole, which is shorter than its diff:
```python
import functools

import jax
import jax.numpy as jnp
from jax import lax
from jax.experimental import pallas as pl
from jax.experimental.pallas import tpu as pltpu
from jax.sharding import PartitionSpec as P

BY_COLS = (((1,), (1,)), ((), ()))
BY_ROWS = (((0,), (0,)), ((), ()))


AHEAD = 3


def layer_kernel(
    experts, groups, pieces, tokens, cotangent, gates, ids, w_in_hbm, w_out_hbm, grad_tokens,
    grad_w, w_in, w_out, table, table_got, raw, sent, passed, got, sums, act, slope, dpre,
    sent_back, got_back, relay_back, relay_sum, far, total, w_own, w_sent, w_got, load_sems,
    table_sems, raw_send, raw_recv, sent_sems, passed_sems, got_sems, back_send, back_recv,
    relay_recv, sum_send, far_sems, w_send, w_recv,
):
    me = lax.axis_index("expert")
    group = lax.axis_index("dp")
    half = experts // 2
    relays = half // 2
    slots = got.shape[2]
    rows = tokens.shape[0]
    columns = grad_w.shape[1]
    per_piece = groups // pieces
    width = per_piece * columns
    turns = 2 * pieces
    my_piece = group // per_piece

    loads = [
        pltpu.make_async_copy(hbm.at[:, pl.ds(p * width, width)], held.at[p], load_sems.at[k, p])
        for k, (hbm, held) in enumerate(((w_in_hbm, w_in), (w_out_hbm, w_out)))
        for p in range(pieces)
    ]
    for load in loads:
        load.start()

    barrier = pltpu.get_barrier_semaphore()

    def greet_expert(step, carry):
        pl.semaphore_signal(barrier, inc=1, device_id={"expert": (me + step) % experts})
        return carry

    def greet_group(step, carry):
        pl.semaphore_signal(barrier, inc=1, device_id={"dp": (group + step) % groups})
        return carry

    lax.fori_loop(1, experts, greet_expert, 0)
    lax.fori_loop(1, groups, greet_group, 0)

    side = me // half
    spot = me % half
    home = side * half
    away = (1 - side) * half
    number = spot % relays
    is_relay = spot // relays == 1 - side
    my_relay = side * relays + (1 - side) * half + number
    home_relays = (1 - side) * relays + side * half

    def peer_of(step):
        return home + (spot + step) % half

    def away_of(u):
        return away + number + u * relays

    def piece_of(turn):
        return (my_piece + 1 + turn) % pieces

    def index_of(turn):
        return (turn // pieces) * pieces + piece_of(turn % pieces)

    def remote(source, dest, send_sem, recv_sem, to):
        return pltpu.make_async_remote_copy(
            src_ref=source,
            dst_ref=dest,
            send_sem=send_sem,
            recv_sem=recv_sem,
            device_id={"expert": to},
        )

    def table_copy(slot, to):
        return remote(table, table_got.at[slot], table_sems.at[2], table_sems.at[slot], to)

    def raw_copy(turn, slot, to):
        part = tokens if turn < pieces else cotangent
        start = pl.multiple_of(piece_of(turn % pieces) * width, width)
        index = index_of(turn)
        return remote(
            part.at[:, pl.ds(start, width)],
            raw.at[slot, index],
            raw_send.at[index],
            raw_recv.at[slot, index],
            to,
        )

    def sent_copy(index, step, slot, to):
        return remote(
            sent.at[index, step],
            got.at[index, slot],
            sent_sems.at[index, step],
            got_sems.at[index, slot],
            to,
        )

    def passed_copy(index, u, step, slot, to):
        return remote(
            passed.at[index, u, step],
            got.at[index, slot],
            passed_sems.at[index, u, step],
            got_sems.at[index, slot],
            to,
        )

    expert_of = lax.broadcasted_iota(jnp.int32, (experts, rows), 0)
    chosen = jnp.zeros((experts, rows), jnp.float32)
    gain = jnp.zeros((experts, rows), jnp.float32)
    for k in range(ids.shape[0]):
        hit = expert_of == ids[k : k + 1, :]
        chosen = chosen + jnp.where(hit, 1.0, 0.0)
        gain = gain + jnp.where(hit, gates[k : k + 1, :], 0.0)
    earlier = jnp.where(
        lax.broadcasted_iota(jnp.int32, (rows, rows), 0)
        < lax.broadcasted_iota(jnp.int32, (rows, rows), 1),
        1.0,
        0.0,
    ).astype(jnp.bfloat16)
    place = jnp.dot(chosen.astype(jnp.bfloat16), earlier, preferred_element_type=jnp.float32)
    table[0] = jnp.where(chosen > 0.0, place, -1.0)
    table[1] = gain
    slot_number = lax.broadcasted_iota(jnp.int32, (slots, rows), 0).astype(jnp.float32)

    def pack(turn, held, expert, part):
        match = slot_number == held[0, pl.ds(expert, 1), :]
        pick = jnp.where(match, 1.0, 0.0).astype(jnp.bfloat16)
        out = jnp.dot(pick, part, preferred_element_type=jnp.float32)
        if turn >= pieces:
            gain_row = held[1, pl.ds(expert, 1), :]
            out = out * jnp.sum(jnp.where(match, gain_row, 0.0), axis=1, keepdims=True)
        return out.astype(jnp.bfloat16)

    def own_part(turn):
        part = tokens if turn < pieces else cotangent
        return part[:, pl.ds(pl.multiple_of(piece_of(turn % pieces) * width, width), width)]

    pl.semaphore_wait(barrier, experts + groups - 2)

    def send(turn):
        index = index_of(turn)
        raw_copy(turn, spot // relays, my_relay).start()

        def to_peer(step, carry):
            to = peer_of(step)
            sent[index, step] = pack(turn, table, to, own_part(turn))
            sent_copy(index, step, me, to).start()
            return carry

        lax.fori_loop(1, half, to_peer, 0)
        got[index, me] = pack(turn, table, me, own_part(turn))

    table_copy(spot // relays, my_relay).start()
    for turn in range(AHEAD):
        send(turn)
    for load in loads:
        load.wait()

    def pass_on(turn):
        index = index_of(turn)
        for u in range(2):
            source = away_of(u)
            if turn == 0:
                table_copy(u, source).wait_recv()
            raw_copy(turn, u, source).wait_recv()

            def to_peer(step, carry):
                to = peer_of(step)
                passed[index, u, step] = pack(turn, table_got.at[u], to, raw[u, index])
                passed_copy(index, u, step, source, to).start()
                return carry

            lax.fori_loop(1, half, to_peer, 0)
            got[index, source] = pack(turn, table_got.at[u], me, raw[u, index])

    def receive(turn):
        index = index_of(turn)

        def from_peer(step, carry):
            source = peer_of(step)
            sent_copy(index, step, source, source).wait_recv()
            return carry

        def from_away(step, carry):
            source = away + step

            def wait():
                passed_copy(index, 0, 0, source, source).wait_recv()

            pl.when(home_relays + step % relays != me)(wait)
            return carry

        lax.fori_loop(1, half, from_peer, 0)
        lax.fori_loop(0, half, from_away, 0)

    def share(to, slot):
        return pltpu.make_async_remote_copy(
            src_ref=w_sent.at[to],
            dst_ref=w_got.at[slot],
            send_sem=w_send.at[to],
            recv_sem=w_recv.at[slot],
            device_id={"dp": to},
        )

    flat = experts * slots
    hidden = act.shape[1]

    def down_part(turn):
        piece = piece_of(turn % pieces)
        down = lax.dot_general(
            act[...],
            got[index_of(turn)].reshape(flat, width),
            BY_ROWS,
            preferred_element_type=jnp.float32,
        ).astype(jnp.bfloat16)
        last = turn == turns - 1
        for u in range(per_piece):
            to = piece * per_piece + u
            w_sent[to] = down[:, u * columns : (u + 1) * columns]
            if not last:
                share(to, group).start()
            elif per_piece > 1:
                pl.when(to != group)(lambda: share(to, group).start())

    for turn in range(turns):
        pl.when(is_relay)(functools.partial(pass_on, turn))
        if turn + AHEAD < turns:
            send(turn + AHEAD)
        receive(turn)
        weights = w_in if turn < pieces else w_out
        part = lax.dot_general(
            got[index_of(turn)].reshape(flat, width),
            weights[piece_of(turn % pieces)],
            BY_COLS,
            preferred_element_type=jnp.float32,
        )
        if turn % pieces > 0:
            part = part + sums[...]
        if turn == pieces - 1:
            sig = 1.0 / (1.0 + jnp.exp(-part))
            act[...] = (part * sig).astype(jnp.bfloat16)
            slope[...] = sig * (1.0 + part * (1.0 - sig))
        elif turn == turns - 1:
            dpre[...] = (part * slope[...]).astype(jnp.bfloat16).reshape(experts, slots, hidden)
        else:
            sums[...] = part
        if pieces <= turn < turns - 1:
            down_part(turn)

    def give_back(source, into):
        for p in range(pieces):
            into[:, p * width : (p + 1) * width] = jnp.dot(
                dpre[source], w_in[p], preferred_element_type=jnp.float32
            ).astype(jnp.bfloat16)

    def relay_copy(source, slot, at, to):
        return remote(
            sent_back.at[source],
            relay_back.at[slot, at],
            back_send.at[source],
            relay_recv.at[slot, at],
            to,
        )

    def back_copy(to, slot):
        return remote(
            sent_back.at[to], got_back.at[slot], back_send.at[to], back_recv.at[slot], to
        )

    def back_away(step, carry):
        source = away + step
        relay = home_relays + step % relays
        slot = step // relays

        def keep():
            give_back(source, relay_back.at[slot, spot])

        def hand():
            give_back(source, sent_back.at[source])
            relay_copy(source, slot, spot, relay).start()

        pl.when(relay == me)(keep)
        pl.when(relay != me)(hand)
        return carry

    lax.fori_loop(0, half, back_away, 0)

    def combine(held, expert, block):
        match = slot_number == held[0, pl.ds(expert, 1), :]
        pick = jnp.where(match, 1.0, 0.0).astype(jnp.bfloat16)
        return lax.dot_general(pick, block, BY_ROWS, preferred_element_type=jnp.float32)

    def far_copy(u, to):
        return remote(relay_sum.at[u], far, sum_send.at[u], far_sems.at[0], to)

    def relay_sums():
        for u in range(2):
            total[...] = combine(table_got.at[u], me, relay_back[u, spot])

            def add(step, carry):
                peer = peer_of(step)
                at = (spot + step) % half
                relay_copy(me, u, at, peer).wait_recv()
                total[...] += combine(table_got.at[u], peer, relay_back[u, at])
                return carry

            lax.fori_loop(1, half, add, 0)
            relay_sum[u] = total[...].astype(jnp.bfloat16)
            far_copy(u, away_of(u)).start()

    pl.when(is_relay)(relay_sums)

    def back_home(step, carry):
        to = peer_of(step)
        give_back(to, sent_back.at[to])
        back_copy(to, me).start()
        return carry

    lax.fori_loop(1, half, back_home, 0)
    give_back(me, got_back.at[me])
    down_part(turns - 1)
    total[...] = combine(table, me, got_back[me])

    w_own[...] = w_sent[group].astype(jnp.float32)

    def gather(step, carry):
        source = (group + step) % groups
        share(source, source).wait_recv()
        w_own[...] += w_got[source].astype(jnp.float32)
        return carry

    lax.fori_loop(1, groups, gather, 0)
    grad_w[...] = w_own[...].astype(jnp.bfloat16)

    def take_back(step, carry):
        source = peer_of(step)
        back_copy(source, source).wait_recv()
        total[...] += combine(table, source, got_back[source])
        return carry

    lax.fori_loop(1, half, take_back, 0)
    far_copy(0, my_relay).wait_recv()
    grad_tokens[...] = (total[...] + far[...].astype(jnp.float32)).astype(jnp.bfloat16)

    table_copy(0, my_relay).wait_send()
    for turn in range(turns):
        index = index_of(turn)
        raw_copy(turn, 0, my_relay).wait_send()

        def drain_sent(step, carry):
            sent_copy(index, step, me, peer_of(step)).wait_send()
            return carry

        def drain_passed(step, carry):
            for u in range(2):
                passed_copy(index, u, step, me, peer_of(step)).wait_send()
            return carry

        lax.fori_loop(1, half, drain_sent, 0)

        def drain_all_passed():
            lax.fori_loop(1, half, drain_passed, 0)

        pl.when(is_relay)(drain_all_passed)

    def drain_away(step, carry):
        relay = home_relays + step % relays

        def wait():
            relay_copy(away + step, 0, 0, relay).wait_send()

        pl.when(relay != me)(wait)
        return carry

    def drain_home(step, carry):
        back_copy(peer_of(step), me).wait_send()
        return carry

    def drain_sums():
        for u in range(2):
            far_copy(u, away_of(u)).wait_send()

    def drain_group(step, carry):
        share((group + step) % groups, group).wait_send()
        return carry

    lax.fori_loop(0, half, drain_away, 0)
    lax.fori_loop(1, half, drain_home, 0)
    pl.when(is_relay)(drain_sums)
    lax.fori_loop(1, groups, drain_group, 0)


def hand_over(first, second, first_out, second_out, first_held, second_held, sems):
    steps = []
    for ref, held, out, which in (
        (first, first_held, first_out, 0),
        (second, second_held, second_out, 1),
    ):
        steps.append(
            (
                pltpu.make_async_copy(ref, held, sems.at[0, which]),
                pltpu.make_async_copy(held, out, sems.at[1, which]),
            )
        )
    for load, _ in steps:
        load.start()
    for load, store in steps:
        load.wait()
        store.start()
    for _, store in steps:
        store.wait()


def per_device(tokens, cotangent, gates, expert_ids, w_in, w_out):
    rows, width = tokens.shape
    hidden = w_out.shape[1]
    experts, groups = lax.axis_size("expert"), lax.axis_size("dp")
    capacity = 5 * rows * expert_ids.shape[1] // (4 * experts)
    slots = -(-capacity // 8) * 8
    columns = width // groups
    pieces = 4 if groups % 4 == 0 else 1
    half, turns, part = experts // 2, 2 * pieces, width // pieces
    shares = pltpu.VMEM((groups, hidden, columns), jnp.bfloat16)
    vmem = pl.BlockSpec(memory_space=pltpu.VMEM)
    anywhere = pl.BlockSpec(memory_space=pl.ANY)
    multiplies = experts * slots * width * hidden
    outs = (
        jax.ShapeDtypeStruct((rows, width), jnp.bfloat16),
        jax.ShapeDtypeStruct((hidden, columns), jnp.bfloat16),
    )
    results = pl.pallas_call(
        functools.partial(layer_kernel, experts, groups, pieces),
        out_shape=outs,
        in_specs=[vmem] * 4 + [anywhere] * 2,
        out_specs=(vmem, vmem),
        scratch_shapes=[
            pltpu.VMEM((pieces, hidden, part), jnp.bfloat16),
            pltpu.VMEM((pieces, hidden, part), jnp.bfloat16),
            pltpu.VMEM((2, experts, rows), jnp.float32),
            pltpu.VMEM((2, 2, experts, rows), jnp.float32),
            pltpu.VMEM((2, turns, rows, part), jnp.bfloat16),
            pltpu.VMEM((turns, half, slots, part), jnp.bfloat16),
            pltpu.VMEM((turns, 2, half, slots, part), jnp.bfloat16),
            pltpu.VMEM((turns, experts, slots, part), jnp.bfloat16),
            pltpu.VMEM((experts * slots, hidden), jnp.float32),
            pltpu.VMEM((experts * slots, hidden), jnp.bfloat16),
            pltpu.VMEM((experts * slots, hidden), jnp.float32),
            pltpu.VMEM((experts, slots, hidden), jnp.bfloat16),
            pltpu.VMEM((experts, slots, width), jnp.bfloat16),
            pltpu.VMEM((experts, slots, width), jnp.bfloat16),
            pltpu.VMEM((2, half, slots, width), jnp.bfloat16),
            pltpu.VMEM((2, rows, width), jnp.bfloat16),
            pltpu.VMEM((rows, width), jnp.bfloat16),
            pltpu.VMEM((rows, width), jnp.float32),
            pltpu.VMEM((hidden, columns), jnp.float32),
            shares,
            shares,
            pltpu.SemaphoreType.DMA((2, pieces)),
            pltpu.SemaphoreType.DMA((3,)),
            pltpu.SemaphoreType.DMA((turns,)),
            pltpu.SemaphoreType.DMA((2, turns)),
            pltpu.SemaphoreType.DMA((turns, half)),
            pltpu.SemaphoreType.DMA((turns, 2, half)),
            pltpu.SemaphoreType.DMA((turns, experts)),
            pltpu.SemaphoreType.DMA((experts,)),
            pltpu.SemaphoreType.DMA((experts,)),
            pltpu.SemaphoreType.DMA((2, half)),
            pltpu.SemaphoreType.DMA((2,)),
            pltpu.SemaphoreType.DMA((1,)),
            pltpu.SemaphoreType.DMA((groups,)),
            pltpu.SemaphoreType.DMA((groups,)),
        ],
        compiler_params=pltpu.CompilerParams(
            collective_id=0, has_side_effects=True, vmem_limit_bytes=56 * 1024 * 1024
        ),
        cost_estimate=pl.CostEstimate(
            flops=8 * multiplies, bytes_accessed=4 * hidden * width, transcendentals=0
        ),
    )(
        tokens,
        cotangent,
        gates.T,
        expert_ids.T,
        jnp.swapaxes(w_in[0], 0, 1),
        w_out[0],
    )
    grad_tokens, grad_w = pl.pallas_call(
        hand_over,
        out_shape=outs,
        in_specs=[anywhere] * 2,
        out_specs=(anywhere, anywhere),
        scratch_shapes=[
            pltpu.VMEM(outs[0].shape, jnp.bfloat16),
            pltpu.VMEM(outs[1].shape, jnp.bfloat16),
            pltpu.SemaphoreType.DMA((2, 2)),
        ],
        compiler_params=pltpu.CompilerParams(vmem_limit_bytes=56 * 1024 * 1024),
    )(*results)
    return grad_tokens, grad_w[None]


def solution(mesh):
    split = P(("expert", "dp"), None)
    whole = P("expert", None, None)
    return jax.shard_map(
        per_device,
        mesh=mesh,
        in_specs=(split, split, split, split, whole, whole),
        out_specs=(split, P("expert", None, "dp")),
        check_vma=False,
    )
```

time: 101 us -> 99.2 us (0.982)
  the two profiles are of different devices: /device:TPU:1 before, /device:TPU:27 now
where the time goes in v4:
time: 99.2 us; the launch traced here: 99 us
  Pallas kernels  98.4 us (99%)
    pallas_call x1, Pallas kernels, per_device(): pl.pallas_call(functools.partial(layer_kernel, experts, groups, pieces),...  96.2 us
    pallas_call x1, Pallas kernels, per_device(): pl.pallas_call(hand_over, out_shape=outs, in_specs=[anywhere] * 2, out_sp...  2.16 us

profile of v4, /device:TPU:27, one launch (start us, length us, event | category | flops | bytes accessed | tf_op | source)
XLA Modules:
  0.0 99.0 jit_solution(8500865306368424446)
XLA Ops:
  0.6 96.2 %shard_map.77 = (bf16[128,2048]{1,0:T(8,128)(2,1)}, bf16[704,512]{1,0:T(8,128)(2,1)}) custom-call(bf16[128,2048]{1,0:T(8,128)(2,1)} %tokens.1, bf16[128,2048]{1,0:T(8,128)(2,1)} %cotangent.1, f32[2,128]{1,0:T(2,128)} %bitcast.10, s32[2,128]{1,0:T(2,128)} %bitcast.11, bf16[704,2048]{1,0:T(8,128)(2,1)} %bitcast.7, bf16[704,2048]{1,0:T(8,128)(2,1)} %bitcast.8), custom_call_target="tpu_custom_call" | custom-call | flops 3690987520 | bytes 5767168 | tf_op jit(solution)/shard_map/pallas_call | solution.py:444
  96.9 2.2 %shard_map.78 = (bf16[128,2048]{1,0:T(8,128)(2,1)}, bf16[704,512]{1,0:T(8,128)(2,1)}) custom-call(bf16[128,2048]{1,0:T(8,128)(2,1)} %get-tuple-element.6.first, bf16[704,512]{1,0:T(8,128)(2,1)} %get-tuple-element.7.second), custom_call_target="tpu_custom_call" | custom-call | tf_op jit(solution)/shard_map/pallas_call | solution.py:500

commit v5 on v4

--- a/solution.py
+++ b/solution.py
@@ -16,10 +16,10 @@
 
 def layer_kernel(
     experts, groups, pieces, tokens, cotangent, gates, ids, w_in_hbm, w_out_hbm, grad_tokens,
-    grad_w, w_in, w_out, table, table_got, raw, sent, passed, got, sums, act, slope, dpre,
-    sent_back, got_back, relay_back, relay_sum, far, total, w_own, w_sent, w_got, load_sems,
-    table_sems, raw_send, raw_recv, sent_sems, passed_sems, got_sems, back_send, back_recv,
-    relay_recv, sum_send, far_sems, w_send, w_recv,
+    grad_w, w_in, w_out, table, table_got, picks, weights_of, raw, sent, passed, got, sums,
+    act, slope, dpre, sent_home, sent_away, got_back, relay_back, relay_sum, far, w_own, w_sent, w_got, load_sems,
+    table_sems, raw_send, raw_recv, sent_sems, passed_sems, got_sems, home_send, away_send,
+    back_recv, relay_recv, sum_send, far_recv, w_send, w_recv,
 ):
     me = lax.axis_index("expert")
     group = lax.axis_index("dp")
@@ -135,14 +135,24 @@
     table[1] = gain
     slot_number = lax.broadcasted_iota(jnp.int32, (slots, rows), 0).astype(jnp.float32)
 
-    def pack(turn, held, expert, part):
-        match = slot_number == held[0, pl.ds(expert, 1), :]
-        pick = jnp.where(match, 1.0, 0.0).astype(jnp.bfloat16)
-        out = jnp.dot(pick, part, preferred_element_type=jnp.float32)
+    def prepare(k, held):
+        for step in range(half):
+            expert = peer_of(step)
+            match = slot_number == held[0, pl.ds(expert, 1), :]
+            picks[k, step] = jnp.where(match, 1.0, 0.0).astype(jnp.bfloat16)
+            gain_row = held[1, pl.ds(expert, 1), :]
+            weights_of[k, step] = jnp.sum(
+                jnp.where(match, gain_row, 0.0), axis=1, keepdims=True
+            )
+
+    def pick_of(k):
+        return picks[k].reshape(half * slots, rows)
+
+    def pack(turn, k, part):
+        out = jnp.dot(pick_of(k), part, preferred_element_type=jnp.float32)
         if turn >= pieces:
-            gain_row = held[1, pl.ds(expert, 1), :]
-            out = out * jnp.sum(jnp.where(match, gain_row, 0.0), axis=1, keepdims=True)
-        return out.astype(jnp.bfloat16)
+            out = out * weights_of[k].reshape(half * slots, 1)
+        return out.astype(jnp.bfloat16).reshape(half, slots, width)
 
     def own_part(turn):
         part = tokens if turn < pieces else cotangent
@@ -154,16 +164,17 @@
         index = index_of(turn)
         raw_copy(turn, spot // relays, my_relay).start()
 
+        sent[index] = pack(turn, 0, own_part(turn))
+
         def to_peer(step, carry):
-            to = peer_of(step)
-            sent[index, step] = pack(turn, table, to, own_part(turn))
-            sent_copy(index, step, me, to).start()
+            sent_copy(index, step, me, peer_of(step)).start()
             return carry
 
         lax.fori_loop(1, half, to_peer, 0)
-        got[index, me] = pack(turn, table, me, own_part(turn))
+        got[index, me] = sent[index, 0]
 
     table_copy(spot // relays, my_relay).start()
+    prepare(0, table)
     for turn in range(AHEAD):
         send(turn)
     for load in loads:
@@ -175,16 +186,17 @@
             source = away_of(u)
             if turn == 0:
                 table_copy(u, source).wait_recv()
+                prepare(1 + u, table_got.at[u])
             raw_copy(turn, u, source).wait_recv()
 
+            passed[index, u] = pack(turn, 1 + u, raw[u, index])
+
             def to_peer(step, carry):
-                to = peer_of(step)
-                passed[index, u, step] = pack(turn, table_got.at[u], to, raw[u, index])
-                passed_copy(index, u, step, source, to).start()
+                passed_copy(index, u, step, source, peer_of(step)).start()
                 return carry
 
             lax.fori_loop(1, half, to_peer, 0)
-            got[index, source] = pack(turn, table_got.at[u], me, raw[u, index])
+            got[index, source] = passed[index, u, 0]
 
     def receive(turn):
         index = index_of(turn)
@@ -260,79 +272,89 @@
         if pieces <= turn < turns - 1:
             down_part(turn)
 
-    def give_back(source, into):
+    def rows_back(first, p):
+        block = dpre[pl.ds(first, half)].reshape(half * slots, hidden)
+        return (
+            jnp.dot(block, w_in[p], preferred_element_type=jnp.float32)
+            .astype(jnp.bfloat16)
+            .reshape(half, slots, width)
+        )
+
+    def relay_copy(p, spot_to, slot, at, to):
+        return remote(
+            sent_away.at[p, spot_to],
+            relay_back.at[p, slot, at],
+            away_send.at[p, spot_to],
+            relay_recv.at[p, slot, at],
+            to,
+        )
+
+    def back_copy(p, spot_to, at, to):
+        return remote(
+            sent_home.at[p, spot_to],
+            got_back.at[p, at],
+            home_send.at[p, spot_to],
+            back_recv.at[p, at],
+            to,
+        )
+
+    def far_copy(p, u, to):
+        return remote(
+            relay_sum.at[p, u], far.at[p], sum_send.at[p, u], far_recv.at[p], to
+        )
+
+    for p in range(pieces):
+        sent_away[p] = rows_back(away, p)
+
+        def back_away(step, carry):
+            relay = home_relays + step % relays
+            slot = step // relays
+
+            def keep():
+                relay_back[p, slot, 0] = sent_away[p, step]
+
+            def hand():
+                at = (spot + half - (relay - home)) % half
+                relay_copy(p, step, slot, at, relay).start()
+
+            pl.when(relay == me)(keep)
+            pl.when(relay != me)(hand)
+            return carry
+
+        lax.fori_loop(0, half, back_away, 0)
+
+    for p in range(pieces):
+        sent_home[p] = rows_back(home, p)
+
+        def back_home(step, carry):
+            back_copy(p, (spot + step) % half, half - step, peer_of(step)).start()
+            return carry
+
+        lax.fori_loop(1, half, back_home, 0)
+        got_back[p, 0] = sent_home[p, spot]
+
+    def combine(k, block):
+        return lax.dot_general(
+            pick_of(k),
+            block.reshape(half * slots, width),
+            BY_ROWS,
+            preferred_element_type=jnp.float32,
+        )
+
+    def relay_sums():
         for p in range(pieces):
-            into[:, p * width : (p + 1) * width] = jnp.dot(
-                dpre[source], w_in[p], preferred_element_type=jnp.float32
-            ).astype(jnp.bfloat16)
-
-    def relay_copy(source, slot, at, to):
-        return remote(
-            sent_back.at[source],
-            relay_back.at[slot, at],
-            back_send.at[source],
-            relay_recv.at[slot, at],
-            to,
-        )
-
-    def back_copy(to, slot):
-        return remote(
-            sent_back.at[to], got_back.at[slot], back_send.at[to], back_recv.at[slot], to
-        )
-
-    def back_away(step, carry):
-        source = away + step
-        relay = home_relays + step % relays
-        slot = step // relays
-
-        def keep():
-            give_back(source, relay_back.at[slot, spot])
-
-        def hand():
-            give_back(source, sent_back.at[source])
-            relay_copy(source, slot, spot, relay).start()
-
-        pl.when(relay == me)(keep)
-        pl.when(relay != me)(hand)
-        return carry
-
-    lax.fori_loop(0, half, back_away, 0)
-
-    def combine(held, expert, block):
-        match = slot_number == held[0, pl.ds(expert, 1), :]
-        pick = jnp.where(match, 1.0, 0.0).astype(jnp.bfloat16)
-        return lax.dot_general(pick, block, BY_ROWS, preferred_element_type=jnp.float32)
-
-    def far_copy(u, to):
-        return remote(relay_sum.at[u], far, sum_send.at[u], far_sems.at[0], to)
-
-    def relay_sums():
-        for u in range(2):
-            total[...] = combine(table_got.at[u], me, relay_back[u, spot])
-
-            def add(step, carry):
-                peer = peer_of(step)
-                at = (spot + step) % half
-                relay_copy(me, u, at, peer).wait_recv()
-                total[...] += combine(table_got.at[u], peer, relay_back[u, at])
-                return carry
-
-            lax.fori_loop(1, half, add, 0)
-            relay_sum[u] = total[...].astype(jnp.bfloat16)
-            far_copy(u, away_of(u)).start()
+            for u in range(2):
+
+                def arrive(step, carry):
+                    relay_copy(p, 0, u, step, me + 1 - 2 * (me % 2)).wait_recv()
+                    return carry
+
+                lax.fori_loop(1, half, arrive, 0)
+                relay_sum[p, u] = combine(1 + u, relay_back[p, u]).astype(jnp.bfloat16)
+                far_copy(p, u, away_of(u)).start()
 
     pl.when(is_relay)(relay_sums)
-
-    def back_home(step, carry):
-        to = peer_of(step)
-        give_back(to, sent_back.at[to])
-        back_copy(to, me).start()
-        return carry
-
-    lax.fori_loop(1, half, back_home, 0)
-    give_back(me, got_back.at[me])
     down_part(turns - 1)
-    total[...] = combine(table, me, got_back[me])
 
     w_own[...] = w_sent[group].astype(jnp.float32)
 
@@ -345,15 +367,18 @@
     lax.fori_loop(1, groups, gather, 0)
     grad_w[...] = w_own[...].astype(jnp.bfloat16)
 
-    def take_back(step, carry):
-        source = peer_of(step)
-        back_copy(source, source).wait_recv()
-        total[...] += combine(table, source, got_back[source])
-        return carry
-
-    lax.fori_loop(1, half, take_back, 0)
-    far_copy(0, my_relay).wait_recv()
-    grad_tokens[...] = (total[...] + far[...].astype(jnp.float32)).astype(jnp.bfloat16)
+    for p in range(pieces):
+
+        def take_back(step, carry):
+            back_copy(p, 0, step, peer_of(step)).wait_recv()
+            return carry
+
+        lax.fori_loop(1, half, take_back, 0)
+        near = combine(0, got_back[p])
+        far_copy(p, 0, my_relay).wait_recv()
+        grad_tokens[:, p * width : (p + 1) * width] = (near + far[p].astype(jnp.float32)).astype(
+            jnp.bfloat16
+        )
 
     table_copy(0, my_relay).wait_send()
     for turn in range(turns):
@@ -380,18 +405,21 @@
         relay = home_relays + step % relays
 
         def wait():
-            relay_copy(away + step, 0, 0, relay).wait_send()
+            for p in range(pieces):
+                relay_copy(p, step, 0, 0, relay).wait_send()
 
         pl.when(relay != me)(wait)
         return carry
 
     def drain_home(step, carry):
-        back_copy(peer_of(step), me).wait_send()
+        for p in range(pieces):
+            back_copy(p, (spot + step) % half, half - step, peer_of(step)).wait_send()
         return carry
 
     def drain_sums():
-        for u in range(2):
-            far_copy(u, away_of(u)).wait_send()
+        for p in range(pieces):
+            for u in range(2):
+                far_copy(p, u, away_of(u)).wait_send()
 
     def drain_group(step, carry):
         share((group + step) % groups, group).wait_send()
@@ -451,6 +479,8 @@
             pltpu.VMEM((pieces, hidden, part), jnp.bfloat16),
             pltpu.VMEM((2, experts, rows), jnp.float32),
             pltpu.VMEM((2, 2, experts, rows), jnp.float32),
+            pltpu.VMEM((3, half, slots, rows), jnp.bfloat16),
+            pltpu.VMEM((3, half, slots, 1), jnp.float32),
             pltpu.VMEM((2, turns, rows, part), jnp.bfloat16),
             pltpu.VMEM((turns, half, slots, part), jnp.bfloat16),
             pltpu.VMEM((turns, 2, half, slots, part), jnp.bfloat16),
@@ -459,12 +489,12 @@
             pltpu.VMEM((experts * slots, hidden), jnp.bfloat16),
             pltpu.VMEM((experts * slots, hidden), jnp.float32),
             pltpu.VMEM((experts, slots, hidden), jnp.bfloat16),
-            pltpu.VMEM((experts, slots, width), jnp.bfloat16),
-            pltpu.VMEM((experts, slots, width), jnp.bfloat16),
-            pltpu.VMEM((2, half, slots, width), jnp.bfloat16),
-            pltpu.VMEM((2, rows, width), jnp.bfloat16),
-            pltpu.VMEM((rows, width), jnp.bfloat16),
-            pltpu.VMEM((rows, width), jnp.float32),
+            pltpu.VMEM((pieces, half, slots, part), jnp.bfloat16),
+            pltpu.VMEM((pieces, half, slots, part), jnp.bfloat16),
+            pltpu.VMEM((pieces, half, slots, part), jnp.bfloat16),
+            pltpu.VMEM((pieces, 2, half, slots, part), jnp.bfloat16),
+            pltpu.VMEM((pieces, 2, rows, part), jnp.bfloat16),
+            pltpu.VMEM((pieces, rows, part), jnp.bfloat16),
             pltpu.VMEM((hidden, columns), jnp.float32),
             shares,
             shares,
@@ -475,11 +505,12 @@
             pltpu.SemaphoreType.DMA((turns, half)),
             pltpu.SemaphoreType.DMA((turns, 2, half)),
             pltpu.SemaphoreType.DMA((turns, experts)),
-            pltpu.SemaphoreType.DMA((experts,)),
-            pltpu.SemaphoreType.DMA((experts,)),
-            pltpu.SemaphoreType.DMA((2, half)),
-            pltpu.SemaphoreType.DMA((2,)),
-            pltpu.SemaphoreType.DMA((1,)),
+            pltpu.SemaphoreType.DMA((pieces, half)),
+            pltpu.SemaphoreType.DMA((pieces, half)),
+            pltpu.SemaphoreType.DMA((pieces, half)),
+            pltpu.SemaphoreType.DMA((pieces, 2, half)),
+            pltpu.SemaphoreType.DMA((pieces, 2)),
+            pltpu.SemaphoreType.DMA((pieces,)),
             pltpu.SemaphoreType.DMA((groups,)),
             pltpu.SemaphoreType.DMA((groups,)),
         ],

time: 99.2 us -> 94.2 us (0.950)
  the two profiles are of different devices: /device:TPU:27 before, /device:TPU:25 now
where the time goes in v5:
time: 94.2 us; the launch traced here: 94 us
  Pallas kernels  93.4 us (99%)
    pallas_call x1, Pallas kernels, per_device(): pl.pallas_call(functools.partial(layer_kernel, experts, groups, pieces),...  91.2 us
    pallas_call x1, Pallas kernels, per_device(): pl.pallas_call(hand_over, out_shape=outs, in_specs=[anywhere] * 2, out_sp...  2.16 us

profile of v5, /device:TPU:25, one launch (start us, length us, event | category | flops | bytes accessed | tf_op | source)
XLA Modules:
  0.0 94.0 jit_solution(15202246021984523128)
XLA Ops:
  0.6 91.2 %shard_map.77 = (bf16[128,2048]{1,0:T(8,128)(2,1)}, bf16[704,512]{1,0:T(8,128)(2,1)}) custom-call(bf16[128,2048]{1,0:T(8,128)(2,1)} %tokens.1, bf16[128,2048]{1,0:T(8,128)(2,1)} %cotangent.1, f32[2,128]{1,0:T(2,128)} %bitcast.10, s32[2,128]{1,0:T(2,128)} %bitcast.11, bf16[704,2048]{1,0:T(8,128)(2,1)} %bitcast.7, bf16[704,2048]{1,0:T(8,128)(2,1)} %bitcast.8), custom_call_target="tpu_custom_call" | custom-call | flops 3690987520 | bytes 5767168 | tf_op jit(solution)/shard_map/pallas_call | solution.py:472
  91.9 2.2 %shard_map.78 = (bf16[128,2048]{1,0:T(8,128)(2,1)}, bf16[704,512]{1,0:T(8,128)(2,1)}) custom-call(bf16[128,2048]{1,0:T(8,128)(2,1)} %get-tuple-element.6.first, bf16[704,512]{1,0:T(8,128)(2,1)} %get-tuple-element.7.second), custom_call_target="tpu_custom_call" | custom-call | tf_op jit(solution)/shard_map/pallas_call | solution.py:531

commit v6 on v5

--- a/solution.py
+++ b/solution.py
@@ -11,7 +11,7 @@
 BY_ROWS = (((0,), (0,)), ((), ()))
 
 
-AHEAD = 3
+AHEAD = 5
 
 
 def layer_kernel(
@@ -25,12 +25,13 @@
     group = lax.axis_index("dp")
     half = experts // 2
     relays = half // 2
-    slots = got.shape[2]
+    slots = got.shape[3]
     rows = tokens.shape[0]
     columns = grad_w.shape[1]
     per_piece = groups // pieces
     width = per_piece * columns
-    turns = 2 * pieces
+    stage = 2 * pieces
+    turns = 2 * stage
     my_piece = group // per_piece
 
     loads = [
@@ -58,22 +59,26 @@
     spot = me % half
     home = side * half
     away = (1 - side) * half
+    mine = spot % 2
     number = spot % relays
     is_relay = spot // relays == 1 - side
-    my_relay = side * relays + (1 - side) * half + number
+    my_relay = side * relays + (1 - side) * half + spot // 2
     home_relays = (1 - side) * relays + side * half
 
     def peer_of(step):
         return home + (spot + step) % half
 
     def away_of(u):
-        return away + number + u * relays
+        return away + 2 * number + u
 
     def piece_of(turn):
         return (my_piece + 1 + turn) % pieces
 
     def index_of(turn):
-        return (turn // pieces) * pieces + piece_of(turn % pieces)
+        return (turn % stage // pieces) * pieces + piece_of(turn % pieces)
+
+    def entry(source):
+        return source // half * relays + source % half // 2
 
     def remote(source, dest, send_sem, recv_sem, to):
         return pltpu.make_async_remote_copy(
@@ -88,7 +93,7 @@
         return remote(table, table_got.at[slot], table_sems.at[2], table_sems.at[slot], to)
 
     def raw_copy(turn, slot, to):
-        part = tokens if turn < pieces else cotangent
+        part = tokens if turn % stage < pieces else cotangent
         start = pl.multiple_of(piece_of(turn % pieces) * width, width)
         index = index_of(turn)
         return remote(
@@ -102,7 +107,7 @@
     def sent_copy(index, step, slot, to):
         return remote(
             sent.at[index, step],
-            got.at[index, slot],
+            got.at[index, slot % 2, entry(slot)],
             sent_sems.at[index, step],
             got_sems.at[index, slot],
             to,
@@ -111,7 +116,7 @@
     def passed_copy(index, u, step, slot, to):
         return remote(
             passed.at[index, u, step],
-            got.at[index, slot],
+            got.at[index, slot % 2, entry(slot)],
             passed_sems.at[index, u, step],
             got_sems.at[index, slot],
             to,
@@ -150,19 +155,19 @@
 
     def pack(turn, k, part):
         out = jnp.dot(pick_of(k), part, preferred_element_type=jnp.float32)
-        if turn >= pieces:
+        if turn % stage >= pieces:
             out = out * weights_of[k].reshape(half * slots, 1)
         return out.astype(jnp.bfloat16).reshape(half, slots, width)
 
     def own_part(turn):
-        part = tokens if turn < pieces else cotangent
+        part = tokens if turn % stage < pieces else cotangent
         return part[:, pl.ds(pl.multiple_of(piece_of(turn % pieces) * width, width), width)]
 
     pl.semaphore_wait(barrier, experts + groups - 2)
 
     def send(turn):
         index = index_of(turn)
-        raw_copy(turn, spot // relays, my_relay).start()
+        raw_copy(turn, mine, my_relay).start()
 
         sent[index] = pack(turn, 0, own_part(turn))
 
@@ -171,52 +176,56 @@
             return carry
 
         lax.fori_loop(1, half, to_peer, 0)
-        got[index, me] = sent[index, 0]
-
-    table_copy(spot // relays, my_relay).start()
+        got[index, mine, entry(me)] = sent[index, 0]
+
+    table_copy(mine, my_relay).start()
     prepare(0, table)
     for turn in range(AHEAD):
-        send(turn)
+        pl.when(mine == turn // stage)(functools.partial(send, turn))
     for load in loads:
         load.wait()
 
     def pass_on(turn):
         index = index_of(turn)
-        for u in range(2):
-            source = away_of(u)
-            if turn == 0:
-                table_copy(u, source).wait_recv()
-                prepare(1 + u, table_got.at[u])
-            raw_copy(turn, u, source).wait_recv()
-
-            passed[index, u] = pack(turn, 1 + u, raw[u, index])
-
-            def to_peer(step, carry):
-                passed_copy(index, u, step, source, peer_of(step)).start()
-                return carry
-
-            lax.fori_loop(1, half, to_peer, 0)
-            got[index, source] = passed[index, u, 0]
+        u = turn // stage
+        source = away_of(u)
+        if turn % stage == 0:
+            table_copy(u, source).wait_recv()
+            prepare(1 + u, table_got.at[u])
+        raw_copy(turn, u, source).wait_recv()
+        passed[index, u] = pack(turn, 1 + u, raw[u, index])
+
+        def to_peer(step, carry):
+            passed_copy(index, u, step, source, peer_of(step)).start()
+            return carry
+
+        lax.fori_loop(1, half, to_peer, 0)
+        got[index, u, entry(source)] = passed[index, u, 0]
 
     def receive(turn):
         index = index_of(turn)
+        u = turn // stage
 
         def from_peer(step, carry):
             source = peer_of(step)
-            sent_copy(index, step, source, source).wait_recv()
+
+            def wait():
+                sent_copy(index, step, source, source).wait_recv()
+
+            pl.when(source % 2 == u)(wait)
             return carry
 
         def from_away(step, carry):
-            source = away + step
+            source = away + 2 * step + u
 
             def wait():
                 passed_copy(index, 0, 0, source, source).wait_recv()
 
-            pl.when(home_relays + step % relays != me)(wait)
+            pl.when(home_relays + step != me)(wait)
             return carry
 
         lax.fori_loop(1, half, from_peer, 0)
-        lax.fori_loop(0, half, from_away, 0)
+        lax.fori_loop(0, relays, from_away, 0)
 
     def share(to, slot):
         return pltpu.make_async_remote_copy(
@@ -227,14 +236,14 @@
             device_id={"dp": to},
         )
 
-    flat = experts * slots
+    flat = half * slots
     hidden = act.shape[1]
 
     def down_part(turn):
         piece = piece_of(turn % pieces)
         down = lax.dot_general(
             act[...],
-            got[index_of(turn)].reshape(flat, width),
+            got[index_of(turn)].reshape(2 * flat, width),
             BY_ROWS,
             preferred_element_type=jnp.float32,
         ).astype(jnp.bfloat16)
@@ -247,53 +256,28 @@
             elif per_piece > 1:
                 pl.when(to != group)(lambda: share(to, group).start())
 
-    for turn in range(turns):
-        pl.when(is_relay)(functools.partial(pass_on, turn))
-        if turn + AHEAD < turns:
-            send(turn + AHEAD)
-        receive(turn)
-        weights = w_in if turn < pieces else w_out
-        part = lax.dot_general(
-            got[index_of(turn)].reshape(flat, width),
-            weights[piece_of(turn % pieces)],
-            BY_COLS,
-            preferred_element_type=jnp.float32,
-        )
-        if turn % pieces > 0:
-            part = part + sums[...]
-        if turn == pieces - 1:
-            sig = 1.0 / (1.0 + jnp.exp(-part))
-            act[...] = (part * sig).astype(jnp.bfloat16)
-            slope[...] = sig * (1.0 + part * (1.0 - sig))
-        elif turn == turns - 1:
-            dpre[...] = (part * slope[...]).astype(jnp.bfloat16).reshape(experts, slots, hidden)
-        else:
-            sums[...] = part
-        if pieces <= turn < turns - 1:
-            down_part(turn)
-
-    def rows_back(first, p):
-        block = dpre[pl.ds(first, half)].reshape(half * slots, hidden)
+    def rows_back(u, first, p):
+        block = dpre[u, pl.ds(first, relays)].reshape(relays * slots, hidden)
         return (
             jnp.dot(block, w_in[p], preferred_element_type=jnp.float32)
             .astype(jnp.bfloat16)
-            .reshape(half, slots, width)
-        )
-
-    def relay_copy(p, spot_to, slot, at, to):
+            .reshape(relays, slots, width)
+        )
+
+    def relay_copy(p, u, step, at, to):
         return remote(
-            sent_away.at[p, spot_to],
-            relay_back.at[p, slot, at],
-            away_send.at[p, spot_to],
-            relay_recv.at[p, slot, at],
+            sent_away.at[p, u, step],
+            relay_back.at[p, u, at],
+            away_send.at[p, u, step],
+            relay_recv.at[p, u, at],
             to,
         )
 
-    def back_copy(p, spot_to, at, to):
+    def back_copy(p, u, step, at, to):
         return remote(
-            sent_home.at[p, spot_to],
+            sent_home.at[p, u, step],
             got_back.at[p, at],
-            home_send.at[p, spot_to],
+            home_send.at[p, u, step],
             back_recv.at[p, at],
             to,
         )
@@ -303,35 +287,44 @@
             relay_sum.at[p, u], far.at[p], sum_send.at[p, u], far_recv.at[p], to
         )
 
-    for p in range(pieces):
-        sent_away[p] = rows_back(away, p)
-
-        def back_away(step, carry):
-            relay = home_relays + step % relays
-            slot = step // relays
-
-            def keep():
-                relay_back[p, slot, 0] = sent_away[p, step]
-
-            def hand():
-                at = (spot + half - (relay - home)) % half
-                relay_copy(p, step, slot, at, relay).start()
-
-            pl.when(relay == me)(keep)
-            pl.when(relay != me)(hand)
-            return carry
-
-        lax.fori_loop(0, half, back_away, 0)
-
-    for p in range(pieces):
-        sent_home[p] = rows_back(home, p)
-
-        def back_home(step, carry):
-            back_copy(p, (spot + step) % half, half - step, peer_of(step)).start()
-            return carry
-
-        lax.fori_loop(1, half, back_home, 0)
-        got_back[p, 0] = sent_home[p, spot]
+    def away_rows(u):
+        for p in range(pieces):
+            sent_away[p, u] = rows_back(u, (1 - side) * relays, p)
+
+            def back_away(step, carry):
+                relay = home_relays + step
+
+                def keep():
+                    relay_back[p, u, 0] = sent_away[p, u, step]
+
+                def hand():
+                    at = (spot + half - (relay - home)) % half
+                    relay_copy(p, u, step, at, relay).start()
+
+                pl.when(relay == me)(keep)
+                pl.when(relay != me)(hand)
+                return carry
+
+            lax.fori_loop(0, relays, back_away, 0)
+
+    def home_rows(u):
+        for p in range(pieces):
+            sent_home[p, u] = rows_back(u, side * relays, p)
+
+            def back_home(step, carry):
+                to = 2 * step + u
+
+                def keep():
+                    got_back[p, 0] = sent_home[p, u, step]
+
+                def hand():
+                    back_copy(p, u, step, (spot + half - to) % half, home + to).start()
+
+                pl.when(to == spot)(keep)
+                pl.when(to != spot)(hand)
+                return carry
+
+            lax.fori_loop(0, relays, back_home, 0)
 
     def combine(k, block):
         return lax.dot_general(
@@ -341,19 +334,53 @@
             preferred_element_type=jnp.float32,
         )
 
-    def relay_sums():
+    def relay_sums(u):
         for p in range(pieces):
-            for u in range(2):
-
-                def arrive(step, carry):
-                    relay_copy(p, 0, u, step, me + 1 - 2 * (me % 2)).wait_recv()
-                    return carry
-
-                lax.fori_loop(1, half, arrive, 0)
-                relay_sum[p, u] = combine(1 + u, relay_back[p, u]).astype(jnp.bfloat16)
-                far_copy(p, u, away_of(u)).start()
-
-    pl.when(is_relay)(relay_sums)
+
+            def arrive(step, carry):
+                relay_copy(p, u, 0, step, peer_of(step)).wait_recv()
+                return carry
+
+            lax.fori_loop(1, half, arrive, 0)
+            relay_sum[p, u] = combine(1 + u, relay_back[p, u]).astype(jnp.bfloat16)
+            far_copy(p, u, away_of(u)).start()
+
+    for turn in range(turns):
+        u = turn // stage
+        pl.when(is_relay)(functools.partial(pass_on, turn))
+        later = turn + AHEAD
+        if later < turns:
+            pl.when(mine == later // stage)(functools.partial(send, later))
+        if turn == turns - 1:
+            pl.when(is_relay)(functools.partial(relay_sums, 0))
+        receive(turn)
+        weights = w_in if turn % stage < pieces else w_out
+        part = lax.dot_general(
+            got[index_of(turn), u].reshape(flat, width),
+            weights[piece_of(turn % pieces)],
+            BY_COLS,
+            preferred_element_type=jnp.float32,
+        )
+        if turn % pieces > 0:
+            part = part + sums[...]
+        if turn % stage == pieces - 1:
+            sig = 1.0 / (1.0 + jnp.exp(-part))
+            act[u * flat : (u + 1) * flat] = (part * sig).astype(jnp.bfloat16)
+            slope[...] = sig * (1.0 + part * (1.0 - sig))
+        elif turn % stage == stage - 1:
+            dpre[u] = (part * slope[...]).astype(jnp.bfloat16).reshape(half, slots, hidden)
+        else:
+            sums[...] = part
+        if stage + pieces <= turn < turns - 1:
+            down_part(turn)
+        if turn == stage + pieces:
+            away_rows(0)
+        if turn == stage + pieces + 1:
+            home_rows(0)
+
+    away_rows(1)
+    home_rows(1)
+    pl.when(is_relay)(functools.partial(relay_sums, 1))
     down_part(turns - 1)
 
     w_own[...] = w_sent[group].astype(jnp.float32)
@@ -370,7 +397,7 @@
     for p in range(pieces):
 
         def take_back(step, carry):
-            back_copy(p, 0, step, peer_of(step)).wait_recv()
+            back_copy(p, 0, 0, step, peer_of(step)).wait_recv()
             return carry
 
         lax.fori_loop(1, half, take_back, 0)
@@ -381,7 +408,7 @@
         )
 
     table_copy(0, my_relay).wait_send()
-    for turn in range(turns):
+    for turn in range(stage):
         index = index_of(turn)
         raw_copy(turn, 0, my_relay).wait_send()
 
@@ -401,19 +428,19 @@
 
         pl.when(is_relay)(drain_all_passed)
 
-    def drain_away(step, carry):
-        relay = home_relays + step % relays
-
-        def wait():
-            for p in range(pieces):
-                relay_copy(p, step, 0, 0, relay).wait_send()
-
-        pl.when(relay != me)(wait)
-        return carry
-
-    def drain_home(step, carry):
-        for p in range(pieces):
-            back_copy(p, (spot + step) % half, half - step, peer_of(step)).wait_send()
+    def drain_back(step, carry):
+        for u in range(2):
+
+            def wait_away():
+                for p in range(pieces):
+                    relay_copy(p, u, step, 0, home_relays + step).wait_send()
+
+            def wait_home():
+                for p in range(pieces):
+                    back_copy(p, u, step, 0, home + 2 * step + u).wait_send()
+
+            pl.when(home_relays + step != me)(wait_away)
+            pl.when(2 * step + u != spot)(wait_home)
         return carry
 
     def drain_sums():
@@ -425,8 +452,7 @@
         share((group + step) % groups, group).wait_send()
         return carry
 
-    lax.fori_loop(0, half, drain_away, 0)
-    lax.fori_loop(1, half, drain_home, 0)
+    lax.fori_loop(0, relays, drain_back, 0)
     pl.when(is_relay)(drain_sums)
     lax.fori_loop(1, groups, drain_group, 0)
 
@@ -484,13 +510,13 @@
             pltpu.VMEM((2, turns, rows, part), jnp.bfloat16),
             pltpu.VMEM((turns, half, slots, part), jnp.bfloat16),
             pltpu.VMEM((turns, 2, half, slots, part), jnp.bfloat16),
-            pltpu.VMEM((turns, experts, slots, part), jnp.bfloat16),
-            pltpu.VMEM((experts * slots, hidden), jnp.float32),
+            pltpu.VMEM((turns, 2, half, slots, part), jnp.bfloat16),
+            pltpu.VMEM((half * slots, hidden), jnp.float32),
             pltpu.VMEM((experts * slots, hidden), jnp.bfloat16),
-            pltpu.VMEM((experts * slots, hidden), jnp.float32),
-            pltpu.VMEM((experts, slots, hidden), jnp.bfloat16),
-            pltpu.VMEM((pieces, half, slots, part), jnp.bfloat16),
-            pltpu.VMEM((pieces, half, slots, part), jnp.bfloat16),
+            pltpu.VMEM((half * slots, hidden), jnp.float32),
+            pltpu.VMEM((2, half, slots, hidden), jnp.bfloat16),
+            pltpu.VMEM((pieces, 2, half // 2, slots, part), jnp.bfloat16),
+            pltpu.VMEM((pieces, 2, half // 2, slots, part), jnp.bfloat16),
             pltpu.VMEM((pieces, half, slots, part), jnp.bfloat16),
             pltpu.VMEM((pieces, 2, half, slots, part), jnp.bfloat16),
             pltpu.VMEM((pieces, 2, rows, part), jnp.bfloat16),
@@ -505,8 +531,8 @@
             pltpu.SemaphoreType.DMA((turns, half)),
             pltpu.SemaphoreType.DMA((turns, 2, half)),
             pltpu.SemaphoreType.DMA((turns, experts)),
-            pltpu.SemaphoreType.DMA((pieces, half)),
-            pltpu.SemaphoreType.DMA((pieces, half)),
+            pltpu.SemaphoreType.DMA((pieces, 2, half // 2)),
+            pltpu.SemaphoreType.DMA((pieces, 2, half // 2)),
             pltpu.SemaphoreType.DMA((pieces, half)),
             pltpu.SemaphoreType.DMA((pieces, 2, half)),
             pltpu.SemaphoreType.DMA((pieces, 2)),

time: 94.2 us -> 103 us (1.093)
  the two profiles are of different devices: /device:TPU:25 before, /device:TPU:31 now
where the time goes in v6:
time: 103 us
  Pallas kernels  102 us (99%)
    pallas_call x1, Pallas kernels, per_device(): pl.pallas_call(functools.partial(layer_kernel, experts, groups, pieces),...  100 us
    pallas_call x1, Pallas kernels, per_device(): pl.pallas_call(hand_over, out_shape=outs, in_specs=[anywhere] * 2, out_sp...  2.16 us

profile of v6, /device:TPU:31, one launch (start us, length us, event | category | flops | bytes accessed | tf_op | source)
XLA Modules:
  0.0 102.9 jit_solution(16613703452810667589)
XLA Ops:
  0.6 100.1 %shard_map.77 = (bf16[128,2048]{1,0:T(8,128)(2,1)}, bf16[704,512]{1,0:T(8,128)(2,1)}) custom-call(bf16[128,2048]{1,0:T(8,128)(2,1)} %tokens.1, bf16[128,2048]{1,0:T(8,128)(2,1)} %cotangent.1, f32[2,128]{1,0:T(2,128)} %bitcast.10, s32[2,128]{1,0:T(2,128)} %bitcast.11, bf16[704,2048]{1,0:T(8,128)(2,1)} %bitcast.7, bf16[704,2048]{1,0:T(8,128)(2,1)} %bitcast.8), custom_call_target="tpu_custom_call" | custom-call | flops 3690987520 | bytes 5767168 | tf_op jit(solution)/shard_map/pallas_call | solution.py:498
  100.8 2.2 %shard_map.78 = (bf16[128,2048]{1,0:T(8,128)(2,1)}, bf16[704,512]{1,0:T(8,128)(2,1)}) custom-call(bf16[128,2048]{1,0:T(8,128)(2,1)} %get-tuple-element.6.first, bf16[704,512]{1,0:T(8,128)(2,1)} %get-tuple-element.7.second), custom_call_target="tpu_custom_call" | custom-call | tf_op jit(solution)/shard_map/pallas_call | solution.py:557

commit v7 on v5

--- a/solution.py
+++ b/solution.py
@@ -323,16 +323,6 @@
 
         lax.fori_loop(0, half, back_away, 0)
 
-    for p in range(pieces):
-        sent_home[p] = rows_back(home, p)
-
-        def back_home(step, carry):
-            back_copy(p, (spot + step) % half, half - step, peer_of(step)).start()
-            return carry
-
-        lax.fori_loop(1, half, back_home, 0)
-        got_back[p, 0] = sent_home[p, spot]
-
     def combine(k, block):
         return lax.dot_general(
             pick_of(k),
@@ -354,6 +344,29 @@
                 far_copy(p, u, away_of(u)).start()
 
     pl.when(is_relay)(relay_sums)
+
+    def drain_away(step, carry):
+        relay = home_relays + step % relays
+
+        def wait():
+            for p in range(pieces):
+                relay_copy(p, step, 0, 0, relay).wait_send()
+
+        pl.when(relay != me)(wait)
+        return carry
+
+    lax.fori_loop(0, half, drain_away, 0)
+
+    for p in range(pieces):
+        sent_home[p] = rows_back(home, p)
+
+        def back_home(step, carry):
+            back_copy(p, (spot + step) % half, half - step, peer_of(step)).start()
+            return carry
+
+        lax.fori_loop(1, half, back_home, 0)
+        got_back[p, 0] = sent_home[p, spot]
+
     down_part(turns - 1)
 
     w_own[...] = w_sent[group].astype(jnp.float32)
@@ -401,16 +414,6 @@
 
         pl.when(is_relay)(drain_all_passed)
 
-    def drain_away(step, carry):
-        relay = home_relays + step % relays
-
-        def wait():
-            for p in range(pieces):
-                relay_copy(p, step, 0, 0, relay).wait_send()
-
-        pl.when(relay != me)(wait)
-        return carry
-
     def drain_home(step, carry):
         for p in range(pieces):
             back_copy(p, (spot + step) % half, half - step, peer_of(step)).wait_send()
@@ -425,7 +428,6 @@
         share((group + step) % groups, group).wait_send()
         return carry
 
-    lax.fori_loop(0, half, drain_away, 0)
     lax.fori_loop(1, half, drain_home, 0)
     pl.when(is_relay)(drain_sums)
     lax.fori_loop(1, groups, drain_group, 0)

time: 94.2 us -> 95.8 us (1.017)
  the two profiles are of different devices: /device:TPU:25 before, /device:TPU:1 now
where the time goes in v7:
time: 95.8 us; the launch traced here: 95.7 us
  Pallas kernels  95 us (99%)
    pallas_call x1, Pallas kernels, per_device(): pl.pallas_call(functools.partial(layer_kernel, experts, groups, pieces),...  92.9 us
    pallas_call x1, Pallas kernels, per_device(): pl.pallas_call(hand_over, out_shape=outs, in_specs=[anywhere] * 2, out_sp...  2.16 us

profile of v7, /device:TPU:1, one launch (start us, length us, event | category | flops | bytes accessed | tf_op | source)
XLA Modules:
  0.0 95.7 jit_solution(16270076343806685737)
XLA Ops:
  0.6 92.9 %shard_map.77 = (bf16[128,2048]{1,0:T(8,128)(2,1)}, bf16[704,512]{1,0:T(8,128)(2,1)}) custom-call(bf16[128,2048]{1,0:T(8,128)(2,1)} %tokens.1, bf16[128,2048]{1,0:T(8,128)(2,1)} %cotangent.1, f32[2,128]{1,0:T(2,128)} %bitcast.10, s32[2,128]{1,0:T(2,128)} %bitcast.11, bf16[704,2048]{1,0:T(8,128)(2,1)} %bitcast.7, bf16[704,2048]{1,0:T(8,128)(2,1)} %bitcast.8), custom_call_target="tpu_custom_call" | custom-call | flops 3690987520 | bytes 5767168 | tf_op jit(solution)/shard_map/pallas_call | solution.py:474
  93.5 2.2 %shard_map.78 = (bf16[128,2048]{1,0:T(8,128)(2,1)}, bf16[704,512]{1,0:T(8,128)(2,1)}) custom-call(bf16[128,2048]{1,0:T(8,128)(2,1)} %get-tuple-element.6.first, bf16[704,512]{1,0:T(8,128)(2,1)} %get-tuple-element.7.second), custom_call_target="tpu_custom_call" | custom-call | tf_op jit(solution)/shard_map/pallas_call | solution.py:533
